TPU v7x, 32 devices: a whole 2x2x4 slice. The times are simulated.
32 devices in a mesh: gx: 8 (over y, x, core), gz: 4 (over z).
Axes of the slice: x: 2, y: 2, z: 4, core: 2. Of those that a mesh axis runs over, the one named last changes fastest.
Arguments:
- tracer: float32 [2, 100, 16, 1024], P(None, 'gz', None, 'gx'), may hold values from -6 to 6
- east_flow: float32 [100, 16, 1024], P('gz', None, 'gx'), may hold values from -0.35 to 0.35
- north_flow: float32 [100, 16, 1024], P('gz', None, 'gx'), may hold values from -0.35 to 0.35
- vertical_flow: float32 [100, 16, 1024], P('gz', None, 'gx'), may hold values from -0.3 to 0.3
- mixing_lateral: float32 [100, 16, 1024], P('gz', None, 'gx'), may hold values from 0.02 to 0.12
- mixing_vertical: float32 [100, 16, 1024], P('gz', None, 'gx'), may hold values from 0.5 to 500
- sea_mask: int32 [100, 16, 1024], P('gz', None, 'gx'), may hold values 0 or 1
- bottom: int32 [16, 1024], P(None, 'gx'), may hold values from 25 to 100
Outputs:
- updated: float32 [2, 100, 16, 1024], P(None, 'gz', None, 'gx')
All inputs are finite; a program needn't handle non-finite values. No bound on the sum of `sea_mask` on one device may be relied on, other than what follows from the above.
Results may differ from a plain program's by a relative error of at most 0.000032.
Values sent between devices are 32-bit elements; how exact they have to be, the bound alone decides.
No kernel may reach another device: no remote copies, remote signals or barrier semaphores. Data moves between devices by JAX's collectives and lax.ppermute only.
A program may use at most 64 MiB of HBM per device.

v0:
```python
import jax
import jax.numpy as jnp
from jax import lax
from jax.sharding import PartitionSpec as P

SUB = 3


def extended_2(array, sides, width, wrap):
    for axis, dim in sides:
        devices, length = (lax.axis_size(axis), array.shape[dim])
        up = [(i, (i + 1) % devices) for i in range(devices if wrap else devices - 1)]
        down = [(j, i) for i, j in up]
        last = lax.slice_in_dim(array, length - width, length, axis=dim)
        initial = lax.slice_in_dim(array, 0, width, axis=dim)
        before = lax.ppermute(last, axis, up)
        after = lax.ppermute(initial, axis, down)
        array = jnp.concatenate([before, array, after], axis=dim)
    return array


def horizontal_step(content, east_speed, diffusion, wet_cells, north_speed):
    west_side = content[..., :-1]
    east_side = content[..., 1:]
    open_faces = wet_cells[..., :-1] * wet_cells[..., 1:]
    flow_east = east_speed[..., :-1]
    flux_east = open_faces * (
        jnp.maximum(flow_east, 0.0) * west_side
        + jnp.minimum(flow_east, 0.0) * east_side
        + 0.5 * (diffusion[..., :-1] + diffusion[..., 1:]) * (west_side - east_side)
    )
    net_east = flux_east[..., 1:] - flux_east[..., :-1]
    interior = content[..., 1:-1]
    wet_inner = wet_cells[..., 1:-1]
    diff_inner = diffusion[..., 1:-1]
    south_side = interior[..., :-1, :]
    north_side = interior[..., 1:, :]
    open_rows = wet_inner[..., :-1, :] * wet_inner[..., 1:, :]
    north_face = north_speed[..., :-1, :]
    flux_north = open_rows * (
        jnp.maximum(north_face, 0.0) * south_side
        + jnp.minimum(north_face, 0.0) * north_side
        + 0.5 * (diff_inner[..., :-1, :] + diff_inner[..., 1:, :]) * (south_side - north_side)
    )
    wall_rows = jnp.zeros_like(flux_north[..., :1, :])
    padded = jnp.concatenate([wall_rows, flux_north, wall_rows], axis=-2)
    net_north = padded[..., 1:, :] - padded[..., :-1, :]
    return interior - wet_inner * (net_east + net_north)


def vertical_step(content, upward, wet_cells):
    upper_cells = content[..., :-1, :, :]
    lower_cells = content[..., 1:, :, :]
    open_faces = wet_cells[:-1] * wet_cells[1:]
    face_speed = upward[:-1]
    flux_up = open_faces * (
        jnp.maximum(face_speed, 0.0) * lower_cells + jnp.minimum(face_speed, 0.0) * upper_cells
    )
    return content[..., 1:-1, :, :] + wet_cells[1:-1] * (
        flux_up[..., 1:, :, :] - flux_up[..., :-1, :, :]
    )


def level_at(array, index):
    return array[..., index, :, :]


def interior_solve(forcing, upper_link, lower_link, diagonal):
    count = diagonal.shape[-3]
    ratios = []
    values = []
    from_above = []
    divisor = level_at(diagonal, 0)
    for level_id in range(count):
        if level_id > 0:
            divisor = level_at(diagonal, level_id) - level_at(upper_link, level_id) * ratios[-1]
            values.append(
                (level_at(forcing, level_id) + level_at(upper_link, level_id) * values[-1])
                / divisor
            )
            from_above.append(level_at(upper_link, level_id) * from_above[-1] / divisor)
        else:
            values.append(level_at(forcing, 0) / divisor)
            from_above.append(level_at(upper_link, 0) / divisor)
        if level_id < count - 1:
            ratios.append(level_at(lower_link, level_id) / divisor)
    from_below_last = level_at(lower_link, count - 1) / divisor
    solved = [values[-1]]
    above_part = [from_above[-1]]
    below_part = [from_below_last]
    for level_id in range(count - 2, -1, -1):
        solved.append(values[level_id] + ratios[level_id] * solved[-1])
        above_part.append(from_above[level_id] + ratios[level_id] * above_part[-1])
        below_part.append(ratios[level_id] * below_part[-1])
    return (
        jnp.stack(solved[::-1], axis=-3),
        jnp.stack(above_part[::-1], axis=-3),
        jnp.stack(below_part[::-1], axis=-3),
    )


def solve_separators(
    start_value,
    start_above,
    start_below,
    end_value,
    end_above,
    end_below,
    rim_forcing,
    rim_upper,
    rim_diagonal,
    rim_lower,
):
    blocks = start_above.shape[0]
    ratios = []
    values = []
    for block_id in range(blocks):
        lower_coef = -rim_upper[block_id] * end_above[block_id]
        centre = rim_diagonal[block_id] - rim_upper[block_id] * end_below[block_id]
        forcing = rim_forcing[:, block_id] + rim_upper[block_id] * end_value[:, block_id]
        if block_id + 1 < blocks:
            centre = centre - rim_lower[block_id] * start_above[block_id + 1]
            forcing = forcing + rim_lower[block_id] * start_value[:, block_id + 1]
            upper_coef = -rim_lower[block_id] * start_below[block_id + 1]
        if block_id > 0:
            divisor = centre - lower_coef * ratios[-1]
            values.append((forcing - lower_coef * values[-1]) / divisor)
        else:
            divisor = centre
            values.append(forcing / divisor)
        if block_id + 1 < blocks:
            ratios.append(upper_coef / divisor)
    solved = [values[-1]]
    for block_id in range(blocks - 2, -1, -1):
        solved.append(values[block_id] - ratios[block_id] * solved[-1])
    return jnp.stack(solved[::-1], axis=1)


def assemble(inner_value, inner_above, inner_below, own_rim, prior_rim):
    inner = (
        inner_value
        + inner_above * prior_rim[..., None, :, :]
        + inner_below * own_rim[..., None, :, :]
    )
    return jnp.concatenate([inner, own_rim[..., None, :, :]], axis=-3)


def column_solve(content, mixing, wet_cells, blocks):
    coupling = mixing[:-1] * wet_cells[:-1] * wet_cells[1:]
    zeroes = jnp.zeros_like(coupling[:1])
    upper_link = jnp.concatenate([zeroes, coupling], axis=0)
    lower_link = jnp.concatenate([coupling, zeroes], axis=0)
    diagonal = 1.0 + upper_link + lower_link
    tracer_count, levels = (content.shape[0], content.shape[1])
    block_levels = levels // blocks
    plane = content.shape[2:]
    forcing = content.reshape((tracer_count, blocks, block_levels) + plane)
    upper_link = upper_link.reshape((blocks, block_levels) + plane)
    lower_link = lower_link.reshape((blocks, block_levels) + plane)
    diagonal = diagonal.reshape((blocks, block_levels) + plane)
    inner = block_levels - 1
    inner_value, inner_above, inner_below = interior_solve(
        forcing[:, :, :inner], upper_link[:, :inner], lower_link[:, :inner], diagonal[:, :inner]
    )
    rims = solve_separators(
        inner_value[:, :, 0],
        inner_above[:, 0],
        inner_below[:, 0],
        inner_value[:, :, inner - 1],
        inner_above[:, inner - 1],
        inner_below[:, inner - 1],
        forcing[:, :, inner],
        upper_link[:, inner],
        diagonal[:, inner],
        lower_link[:, inner],
    )
    prior = jnp.concatenate([jnp.zeros_like(rims[:, :1]), rims[:, :-1]], axis=1)
    solved = assemble(inner_value, inner_above, inner_below, rims, prior)
    return solved.reshape(content.shape)


def settle_mix(pieces, blocks):
    content, coefficients = pieces
    mixed_out = column_solve(content, coefficients[0], coefficients[1], blocks)
    return lax.all_to_all(mixed_out, "gz", split_axis=1, concat_axis=2, tiled=True)


def local(
    tracer, east_flow, north_flow, vertical_flow, mixing_lateral, mixing_vertical, sea_mask, bottom
):
    levels_here = tracer.shape[1]
    tracer_count = tracer.shape[0]
    blocks = lax.axis_size("gz")
    level_index = lax.axis_index("gz") * levels_here + lax.broadcasted_iota(
        jnp.int32, sea_mask.shape, 0
    )
    wet_cells = sea_mask.astype(jnp.float32) * (level_index < bottom[None]).astype(jnp.float32)
    tracers_now = tracer
    statics = extended_2(jnp.stack([east_flow, mixing_lateral, wet_cells]), (("gx", 3),), 1, True)
    for substep in range(SUB):
        extended = extended_2(tracers_now, (("gx", 3),), 1, True)
        tracers_now = horizontal_step(extended, statics[0], statics[1], statics[2], north_flow)
    stacked = jnp.concatenate([tracers_now, vertical_flow[None], wet_cells[None]], axis=0)
    extended = extended_2(stacked, (("gz", 1),), 1, False)
    tracers_now = vertical_step(
        extended[:tracer_count], extended[tracer_count], extended[tracer_count + 1]
    )
    coefficients = jnp.stack([mixing_vertical, wet_cells])
    result = settle_mix(
        (
            lax.all_to_all(tracers_now, "gz", split_axis=2, concat_axis=1, tiled=True),
            lax.all_to_all(coefficients, "gz", split_axis=2, concat_axis=1, tiled=True),
        ),
        blocks=blocks,
    )
    return result


def solution(mesh):
    return jax.shard_map(
        local,
        mesh=mesh,
        in_specs=(
            P(None, "gz", None, "gx"),
            P("gz", None, "gx"),
            P("gz", None, "gx"),
            P("gz", None, "gx"),
            P("gz", None, "gx"),
            P("gz", None, "gx"),
            P("gz", None, "gx"),
            P(None, "gx"),
        ),
        out_specs=P(None, "gz", None, "gx"),
        check_vma=False,
    )
```

profile of v0, /device:TPU:0, one launch (start us, length us, event | category | flops | bytes accessed | tf_op | source)
XLA Modules:
  0.0 124.4 jit_solution(6703661857384951737)
XLA Ops:
  0.8 1.5 %copy.904 = s32[25,16,128]{0,1,2:T(8,128)S(1)} copy(s32[25,16,128]{2,1,0:T(8,128)} %param.14) | data formatting | bytes 409600 | tf_op args[6]
  2.3 2.4 %copy.901 = f32[25,16,128]{0,1,2:T(8,128)} copy(f32[25,16,128]{2,1,0:T(8,128)} %param.9) | data formatting | bytes 409600 | tf_op args[1]
  4.7 1.5 %copy.902 = f32[25,16,128]{0,1,2:T(8,128)} copy(f32[25,16,128]{2,1,0:T(8,128)S(1)} %copy-done.7) | data formatting | bytes 409600 | tf_op args[4]
  8.0 1.6 %copy-done = f32[3,25,16,128]{1,2,3,0:T(8,128)} copy-done((f32[3,25,16,128]{1,2,3,0:T(8,128)}, f32[3,25,16,128]{1,2,3,0:T(8,128)S(1)}, u32[]{:S(2)}) %copy-start) | copy-done | bytes 614424
  10.7 2.9 %collective-permute-start.1 = (f32[3,25,16,1]{1,2,3,0:T(8,128)}, f32[3,25,16,1]{1,2,3,0:T(8,128)S(1)}, u32[]{:S(2)}, u32[]{:S(2)}) collective-permute-start(f32[3,25,16,1]{1,2,3,0:T(8,128)} %get-tuple-element.177), channel_id=1, source_target_pairs={{4,0},{8,4},{12,8},{16,12},{20,16},{24,20},{28,24},{0,28},{5,1},{9... | collective-permute-start | bytes 14408 | tf_op jit(solution)/shard_map/ppermute | solution.py:17
  14.1 1.4 %pad_maximum_fusion.1 = f32[2,25,16,128]{1,2,3,0:T(8,128)} fusion(f32[1,25,16,128]{1,2,3,0:T(8,128)S(1)} %fusion.126, f32[1,25,16,128]{1,2,3,0:T(8,128)S(1)} %bitcast.1683), kind=kLoop, calls=%fused_computation.1 | loop fusion | flops 102400 | bytes 819200 | tf_op jit(solution)/shard_map/stack | solution.py:208
  15.6 2.6 %copy.929 = f32[2,25,16,128]{3,0,1,2:T(2,128)} copy(f32[2,25,16,128]{1,2,3,0:T(8,128)} %pad_maximum_fusion.1) | data formatting | bytes 819200 | tf_op jit(solution)/shard_map/stack | solution.py:208
  18.2 5.6 %all-to-all-start.1 = ((f32[2,25,16,128]{3,0,1,2:T(2,128)}), f32[2,25,16,128]{3,0,1,2:T(2,128)}, u32[]{:S(2)}, u32[]{:S(2)}) async-start(f32[2,25,16,128]{3,0,1,2:T(2,128)} %copy.929), calls=%async_computation.1 | async-start | bytes 819200 | tf_op jit(solution)/shard_map/all_to_all | solution.py:212
  26.0 2.6 %collective-permute-start.3 = (f32[2,25,16,1]{3,1,0,2:T(8,128)}, f32[2,25,16,1]{3,1,0,2:T(8,128)}, u32[]{:S(2)}, u32[]{:S(2)}) collective-permute-start(f32[2,25,16,1]{3,1,0,2:T(8,128)} %get-tuple-element.189), channel_id=1, source_target_pairs={{4,0},{8,4},{12,8},{16,12},{20,16},{24,20},{28,24},{0,28},{5,1},{9... | collective-permute-start | bytes 9608 | tf_op jit(solution)/shard_map/ppermute | solution.py:17
  29.8 2.5 %copy.906 = f32[3,25,16,128]{3,2,1,0:T(8,128)S(1)} copy(f32[3,25,16,128]{1,2,3,0:T(8,128)} %copy-done) | data formatting | bytes 1228800 | tf_op jit(solution)/shard_map/stack | solution.py:199
  32.5 6.1 %collective-permute-done.3 = f32[2,25,16,1]{3,1,0,2:T(8,128)} collective-permute-done((f32[2,25,16,1]{3,1,0,2:T(8,128)}, f32[2,25,16,1]{3,1,0,2:T(8,128)}, u32[]{:S(2)}, u32[]{:S(2)}) %collective-permute-start.3) | collective-permute-done | bytes 3232 | tf_op jit(solution)/shard_map/ppermute | solution.py:17
  38.6 1.9 %constant_dynamic-update-slice_fusion = f32[2,25,16,129]{3,1,0,2:T(8,128)} fusion(f32[2,25,16,129]{3,1,0,2:T(8,128)} %get-tuple-element.197, f32[2,25,16,1]{3,1,0,2:T(8,128)} %collective-permute-done.3), kind=kLoop, calls=%fused_computation.66 | loop fusion | bytes 1048576 | tf_op jit(solution)/shard_map/concatenate | solution.py:18
  40.5 1.2 copy.907
  43.0 1.8 %pad_maximum_fusion.2 = f32[3,25,16,130]{3,2,1,0:T(8,128)S(1)} fusion(f32[3,25,16,1]{3,2,1,0:T(8,128)} %copy.907, f32[3,25,16,128]{3,2,1,0:T(8,128)S(1)} %copy.906, f32[3,25,16,1]{3,2,1,0:T(8,128)} %copy.905), kind=kLoop, calls=%fused_computation.2 | loop fusion | flops 312000 | bytes 1248000 | tf_op jit(solution)/shard_map/concatenate | solution.py:18
  47.3 1.7 %add_multiply_fusion.2 = f32[2,25,16,129]{3,1,0,2:T(8,128)S(1)} fusion(f32[2,25,16,129]{3,1,0,2:T(8,128)S(1)} %copy-done.3, f32[2,25,16,128]{3,1,0,2:T(8,128)S(1)} %get-tuple-element.196, f32[2,25,16,1]{3,1,0,2:T(8,128)} %collective-permute-done.2, f32[25,16,129]{2,0,1:T(8,128)S(1)} %copy.916, f32[25,16,129]{2,0,1:T(8,128)S(1)} %copy.913, ...), kind=kLoop, calls=%fused_computation.10 | loop fusion | flops 825600 | bytes 2064000 | tf_op jit(solution)/shard_map/mul | solution.py:27
  49.5 2.6 %collective-permute-start.4 = (f32[2,25,16,1]{3,1,0,2:T(8,128)S(1)}, f32[2,25,16,1]{3,1,0,2:T(8,128)S(1)}, u32[]{:S(2)}, u32[]{:S(2)}) collective-permute-start(f32[2,25,16,1]{3,1,0,2:T(8,128)S(1)} %get-tuple-element.186), channel_id=1, source_target_pairs={{0,4},{4,8},{8,12},{12,16},{16,20},{20,24},{24,28},{28,0},{1,5},{5... | collective-permute-start | bytes 9608 | tf_op jit(solution)/shard_map/ppermute | solution.py:16
  52.6 10.1 %collective-permute-done.4 = f32[2,25,16,1]{3,1,0,2:T(8,128)S(1)} collective-permute-done((f32[2,25,16,1]{3,1,0,2:T(8,128)S(1)}, f32[2,25,16,1]{3,1,0,2:T(8,128)S(1)}, u32[]{:S(2)}, u32[]{:S(2)}) %collective-permute-start.4) | collective-permute-done | bytes 3232 | tf_op jit(solution)/shard_map/ppermute | solution.py:16
  65.8 1.9 %collective-permute-start.7 = (f32[2,25,16,1]{3,1,0,2:T(8,128)S(1)}, f32[2,25,16,1]{3,1,0,2:T(8,128)S(1)}, u32[]{:S(2)}, u32[]{:S(2)}) collective-permute-start(f32[2,25,16,1]{3,1,0,2:T(8,128)S(1)} %get-tuple-element.185), channel_id=1, source_target_pairs={{4,0},{8,4},{12,8},{16,12},{20,16},{24,20},{28,24},{0,28},{5,1},{9... | collective-permute-start | bytes 9608 | tf_op jit(solution)/shard_map/ppermute | solution.py:17
  67.9 11.6 %collective-permute-done.6 = f32[2,25,16,1]{3,1,0,2:T(8,128)S(1)} collective-permute-done((f32[2,25,16,1]{3,1,0,2:T(8,128)S(1)}, f32[2,25,16,1]{3,1,0,2:T(8,128)S(1)}, u32[]{:S(2)}, u32[]{:S(2)}) %collective-permute-start.6) | collective-permute-done | bytes 3232 | tf_op jit(solution)/shard_map/ppermute | solution.py:16
  80.3 1.3 %collective-permute-start.9 = (f32[4,1,16,128]{3,1,0,2:T(1,128)S(1)}, f32[4,1,16,128]{3,1,0,2:T(1,128)S(1)}, u32[]{:S(2)}, u32[]{:S(2)}) collective-permute-start(f32[4,1,16,128]{3,1,0,2:T(1,128)S(1)} %get-tuple-element.182), channel_id=1, source_target_pairs={{1,0},{2,1},{3,2},{5,4},{6,5},{7,6},{9,8},{10,9},{11,10},{13,12},{... | collective-permute-start | bytes 98312 | tf_op jit(solution)/shard_map/ppermute | solution.py:17
  81.6 4.7 %collective-permute-start.8 = (f32[4,1,16,128]{3,1,0,2:T(1,128)S(1)}, f32[4,1,16,128]{3,1,0,2:T(1,128)S(1)}, u32[]{:S(2)}, u32[]{:S(2)}) collective-permute-start(f32[4,1,16,128]{3,1,0,2:T(1,128)S(1)} %get-tuple-element.183), channel_id=1, source_target_pairs={{0,1},{1,2},{2,3},{4,5},{5,6},{6,7},{8,9},{9,10},{10,11},{12,13},{... | collective-permute-start | bytes 98312 | tf_op jit(solution)/shard_map/ppermute | solution.py:16
  89.1 5.9 %all-to-all-start = ((f32[2,25,16,128]{3,1,0,2:T(8,128)}), f32[2,25,16,128]{3,1,0,2:T(8,128)S(1)}, u32[]{:S(2)}, u32[]{:S(2)}) async-start(f32[2,25,16,128]{3,1,0,2:T(8,128)} %fusion.1), calls=%async_computation | async-start | bytes 1048576 | tf_op jit(solution)/shard_map/all_to_all | solution.py:211
  97.9 10.4 %all-to-all-done = f32[2,25,16,128]{3,1,0,2:T(8,128)S(1)} async-done(((f32[2,25,16,128]{3,1,0,2:T(8,128)}), f32[2,25,16,128]{3,1,0,2:T(8,128)S(1)}, u32[]{:S(2)}, u32[]{:S(2)}) %all-to-all-start) | async-done | bytes 409632 | tf_op jit(solution)/shard_map/all_to_all | solution.py:211
  109.8 13.7 %all_to_all.48 = f32[2,100,4,128]{3,2,0,1:T(4,128)S(1)} all-to-all(f32[2,100,4,128]{3,2,0,1:T(4,128)S(1)} %copy.1096), channel_id=1, replica_groups=mesh['gx'=8,'gz'=4] {'gz'}, dimensions={1} | all-to-all | bytes 819200 | tf_op jit(solution)/shard_map/all_to_all | solution.py:185
  (157 shorter events, 24.2 us)
Async XLA Ops:
  0.0 4.7 %copy-start.7 = (f32[25,16,128]{2,1,0:T(8,128)S(1)}, f32[25,16,128]{2,1,0:T(8,128)}, u32[]{:S(2)}) copy-start(f32[25,16,128]{2,1,0:T(8,128)} %param.12) | copy-start | bytes 614404
  6.1 1.2 copy-start.1
  6.2 1.5 %copy-start.2 = (f32[25,16,128]{0,1,2:T(8,128)S(1)}, f32[25,16,128]{0,1,2:T(8,128)}, u32[]{:S(2)}) copy-start(f32[25,16,128]{0,1,2:T(8,128)} %copy.902) | copy-start | bytes 614404
  7.7 5.9 %copy-start.8 = (f32[25,16,128]{2,1,0:T(8,128)S(1)}, f32[25,16,128]{2,1,0:T(8,128)}, u32[]{:S(2)}) copy-start(f32[25,16,128]{2,1,0:T(8,128)} %param.13) | copy-start | bytes 614404
  8.0 1.6 %copy-start = (f32[3,25,16,128]{1,2,3,0:T(8,128)}, f32[3,25,16,128]{1,2,3,0:T(8,128)S(1)}, u32[]{:S(2)}) copy-start(f32[3,25,16,128]{1,2,3,0:T(8,128)S(1)} %pad_maximum_fusion) | copy-start | bytes 1843204
  10.3 31.5 %collective-permute-start = (f32[3,25,16,1]{1,2,3,0:T(8,128)S(1)}, f32[3,25,16,1]{1,2,3,0:T(8,128)S(1)}, u32[]{:S(2)}, u32[]{:S(2)}) collective-permute-start(f32[3,25,16,1]{1,2,3,0:T(8,128)S(1)} %get-tuple-element.176), channel_id=1, source_target_pairs={{0,4},{4,8},{8,12},{12,16},{16,20},{20,24},{24,28},{28,0},{1,5},{5... | collective-permute-start | bytes 14408 | tf_op jit(solution)/shard_map/ppermute | solution.py:16
  10.7 29.8 %collective-permute-start.1 = (f32[3,25,16,1]{1,2,3,0:T(8,128)}, f32[3,25,16,1]{1,2,3,0:T(8,128)S(1)}, u32[]{:S(2)}, u32[]{:S(2)}) collective-permute-start(f32[3,25,16,1]{1,2,3,0:T(8,128)} %get-tuple-element.177), channel_id=1, source_target_pairs={{4,0},{8,4},{12,8},{16,12},{20,16},{24,20},{28,24},{0,28},{5,1},{9... | collective-permute-start | bytes 14408 | tf_op jit(solution)/shard_map/ppermute | solution.py:17
  15.6 8.3 %copy-start.4 = (f32[2,25,16,128]{3,2,1,0:T(8,128)S(1)}, f32[2,25,16,128]{3,2,1,0:T(8,128)}, u32[]{:S(2)}) copy-start(f32[2,25,16,128]{3,2,1,0:T(8,128)} %param.8) | copy-start | bytes 1228804
  18.2 70.8 %all-to-all-start.1 = ((f32[2,25,16,128]{3,0,1,2:T(2,128)}), f32[2,25,16,128]{3,0,1,2:T(2,128)}, u32[]{:S(2)}, u32[]{:S(2)}) async-start(f32[2,25,16,128]{3,0,1,2:T(2,128)} %copy.929), calls=%async_computation.1 | async-start | bytes 819200 | tf_op jit(solution)/shard_map/all_to_all | solution.py:212
  23.8 4.8 %copy-start.10 = (f32[25,16,128]{2,1,0:T(8,128)S(1)}, f32[25,16,128]{2,1,0:T(8,128)}, u32[]{:S(2)}) copy-start(f32[25,16,128]{2,1,0:T(8,128)} %param.10) | copy-start | bytes 614404
  26.0 21.2 %collective-permute-start.2 = (f32[2,25,16,1]{3,1,0,2:T(8,128)}, f32[2,25,16,1]{3,1,0,2:T(8,128)}, u32[]{:S(2)}, u32[]{:S(2)}) collective-permute-start(f32[2,25,16,1]{3,1,0,2:T(8,128)} %get-tuple-element.188), channel_id=1, source_target_pairs={{0,4},{4,8},{8,12},{12,16},{16,20},{20,24},{24,28},{28,0},{1,5},{5... | collective-permute-start | bytes 9608 | tf_op jit(solution)/shard_map/ppermute | solution.py:16
  26.0 12.6 %collective-permute-start.3 = (f32[2,25,16,1]{3,1,0,2:T(8,128)}, f32[2,25,16,1]{3,1,0,2:T(8,128)}, u32[]{:S(2)}, u32[]{:S(2)}) collective-permute-start(f32[2,25,16,1]{3,1,0,2:T(8,128)} %get-tuple-element.189), channel_id=1, source_target_pairs={{4,0},{8,4},{12,8},{16,12},{20,16},{24,20},{28,24},{0,28},{5,1},{9... | collective-permute-start | bytes 9608 | tf_op jit(solution)/shard_map/ppermute | solution.py:17
  29.8 2.5 %copy-start.9 = (f32[25,16,128]{2,1,0:T(8,128)S(1)}, f32[25,16,128]{2,1,0:T(8,128)}, u32[]{:S(2)}) copy-start(f32[25,16,128]{2,1,0:T(8,128)} %param.11) | copy-start | bytes 614404
  29.8 2.6 %copy-start.6 = (f32[25,15,128]{2,1,0:T(8,128)S(1)}, f32[25,15,128]{2,1,0:T(8,128)}, u32[]{:S(2)}) copy-start(f32[25,15,128]{2,1,0:T(8,128)} %get-tuple-element.232) | copy-start | bytes 576004
  46.1 1.2 copy-start.3
  47.1 1.8 %copy-start.5 = (f32[2,25,16,128]{3,2,1,0:T(8,128)S(1)}, f32[2,25,16,128]{3,2,1,0:T(8,128)}, u32[]{:S(2)}) copy-start(f32[2,25,16,128]{3,2,1,0:T(8,128)} %param.8) | copy-start | bytes 1228804
  49.5 13.2 %collective-permute-start.4 = (f32[2,25,16,1]{3,1,0,2:T(8,128)S(1)}, f32[2,25,16,1]{3,1,0,2:T(8,128)S(1)}, u32[]{:S(2)}, u32[]{:S(2)}) collective-permute-start(f32[2,25,16,1]{3,1,0,2:T(8,128)S(1)} %get-tuple-element.186), channel_id=1, source_target_pairs={{0,4},{4,8},{8,12},{12,16},{16,20},{20,24},{24,28},{28,0},{1,5},{5... | collective-permute-start | bytes 9608 | tf_op jit(solution)/shard_map/ppermute | solution.py:16
  52.1 11.6 %collective-permute-start.5 = (f32[2,25,16,1]{3,1,0,2:T(8,128)S(1)}, f32[2,25,16,1]{3,1,0,2:T(8,128)S(1)}, u32[]{:S(2)}, u32[]{:S(2)}) collective-permute-start(f32[2,25,16,1]{3,1,0,2:T(8,128)S(1)} %get-tuple-element.187), channel_id=1, source_target_pairs={{4,0},{8,4},{12,8},{16,12},{20,16},{24,20},{28,24},{0,28},{5,1},{9... | collective-permute-start | bytes 9608 | tf_op jit(solution)/shard_map/ppermute | solution.py:17
  64.7 14.7 %collective-permute-start.6 = (f32[2,25,16,1]{3,1,0,2:T(8,128)S(1)}, f32[2,25,16,1]{3,1,0,2:T(8,128)S(1)}, u32[]{:S(2)}, u32[]{:S(2)}) collective-permute-start(f32[2,25,16,1]{3,1,0,2:T(8,128)S(1)} %get-tuple-element.184), channel_id=1, source_target_pairs={{0,4},{4,8},{8,12},{12,16},{16,20},{20,24},{24,28},{28,0},{1,5},{5... | collective-permute-start | bytes 9608 | tf_op jit(solution)/shard_map/ppermute | solution.py:16
  65.8 13.6 %collective-permute-start.7 = (f32[2,25,16,1]{3,1,0,2:T(8,128)S(1)}, f32[2,25,16,1]{3,1,0,2:T(8,128)S(1)}, u32[]{:S(2)}, u32[]{:S(2)}) collective-permute-start(f32[2,25,16,1]{3,1,0,2:T(8,128)S(1)} %get-tuple-element.185), channel_id=1, source_target_pairs={{4,0},{8,4},{12,8},{16,12},{20,16},{24,20},{28,24},{0,28},{5,1},{9... | collective-permute-start | bytes 9608 | tf_op jit(solution)/shard_map/ppermute | solution.py:17
  80.3 6.8 %collective-permute-start.9 = (f32[4,1,16,128]{3,1,0,2:T(1,128)S(1)}, f32[4,1,16,128]{3,1,0,2:T(1,128)S(1)}, u32[]{:S(2)}, u32[]{:S(2)}) collective-permute-start(f32[4,1,16,128]{3,1,0,2:T(1,128)S(1)} %get-tuple-element.182), channel_id=1, source_target_pairs={{1,0},{2,1},{3,2},{5,4},{6,5},{7,6},{9,8},{10,9},{11,10},{13,12},{... | collective-permute-start | bytes 98312 | tf_op jit(solution)/shard_map/ppermute | solution.py:17
  81.6 6.1 %collective-permute-start.8 = (f32[4,1,16,128]{3,1,0,2:T(1,128)S(1)}, f32[4,1,16,128]{3,1,0,2:T(1,128)S(1)}, u32[]{:S(2)}, u32[]{:S(2)}) collective-permute-start(f32[4,1,16,128]{3,1,0,2:T(1,128)S(1)} %get-tuple-element.183), channel_id=1, source_target_pairs={{0,1},{1,2},{2,3},{4,5},{5,6},{6,7},{8,9},{9,10},{10,11},{12,13},{... | collective-permute-start | bytes 98312 | tf_op jit(solution)/shard_map/ppermute | solution.py:16
  89.1 19.3 %all-to-all-start = ((f32[2,25,16,128]{3,1,0,2:T(8,128)}), f32[2,25,16,128]{3,1,0,2:T(8,128)S(1)}, u32[]{:S(2)}, u32[]{:S(2)}) async-start(f32[2,25,16,128]{3,1,0,2:T(8,128)} %fusion.1), calls=%async_computation | async-start | bytes 1048576 | tf_op jit(solution)/shard_map/all_to_all | solution.py:211
where the time goes:
time: 125 us; the launch traced here: 124 us
  waiting for transfers between devices  39.8 us (32%)
  starting transfers between devices  29.4 us (24%)
  local copies, waits for them, and re-layouts  27.4 us (22%)
  blocking collectives  13.7 us (11%)
  other arithmetic  13.4 us (11%)
    ppermute x5, waiting for transfers between devices, extended_2(): before = lax.ppermute(last, axis, up)  22.2 us
    all_to_all x1, blocking collectives, settle_mix(): lax.all_to_all(mixed_out, 'gz', split_axis=1, concat_axis=2, tiled=True)  13.7 us
    unnamed x60, local copies, waits for them, and re-layouts  11 us
    all_to_all x1, waiting for transfers between devices, local(): lax.all_to_all(tracers_now, 'gz', split_axis=2, concat_axis=1, tiled=True)  10.4 us
    ppermute x5, starting transfers between devices, extended_2(): after = lax.ppermute(initial, axis, down)  9.03 us
    ppermute x5, starting transfers between devices, extended_2(): before = lax.ppermute(last, axis, up)  8.83 us
    ppermute x5, waiting for transfers between devices, extended_2(): after = lax.ppermute(initial, axis, down)  7.16 us
    all_to_all x1, starting transfers between devices, local(): lax.all_to_all(tracers_now, 'gz', split_axis=2, concat_axis=1, tiled=True)  5.93 us
  transfers between devices with their start and end apart: 12, of which 6 were waited for; matrix products, arithmetic and copies ran while one was open for 23% of the time, Pallas kernels for 0%

commit v1 on v0

v1 whole, which is shorter than its diff:
```python
import functools

import jax
import jax.numpy as jnp
from jax import lax
from jax.experimental import pallas as pl
from jax.experimental.pallas import tpu as pltpu
from jax.sharding import PartitionSpec as P

SUB = 3
SLOT = 3 * SUB
GROUP = SLOT // SUB

VMEM = pl.BlockSpec(memory_space=pltpu.VMEM)


def call(kernel, shapes, flops, *operands):
    outs = [jax.ShapeDtypeStruct(s, jnp.float32) for s in shapes]
    size = sum(o.size * o.dtype.itemsize for o in (*operands, *outs))
    return pl.pallas_call(
        kernel,
        out_shape=outs,
        in_specs=[VMEM] * len(operands),
        out_specs=[VMEM] * len(outs),
        compiler_params=pltpu.CompilerParams(vmem_limit_bytes=24 * 2**20),
        cost_estimate=pl.CostEstimate(flops=flops, bytes_accessed=size, transcendentals=0),
    )(*operands)


def rolled(plane, shift, axis):
    return pltpu.roll(plane, shift % plane.shape[axis], axis)


def lanes_of(plane):
    return lax.broadcasted_iota(jnp.int32, plane.shape, 1)


def wetness(mask_ref, bottom, level, first_level):
    return jnp.where((mask_ref[level] > 0) & (first_level + level < bottom), 1.0, 0.0)


def lateral_coefficients(east, north, mixing, wet):
    rows = east.shape[0]
    open_east = wet * rolled(wet, -1, 1)
    mean_east = 0.5 * (mixing + rolled(mixing, -1, 1))
    row = lax.broadcasted_iota(jnp.int32, wet.shape, 0)
    open_north = jnp.where(row < rows - 1, wet * rolled(wet, -1, 0), 0.0)
    mean_north = 0.5 * (mixing + rolled(mixing, -1, 0))
    return (
        open_east * (jnp.maximum(east, 0.0) + mean_east),
        open_east * (jnp.minimum(east, 0.0) - mean_east),
        open_north * (jnp.maximum(north, 0.0) + mean_north),
        open_north * (jnp.minimum(north, 0.0) - mean_north),
    )


def lateral_substeps(content, coefficients):
    from_here, from_east, from_row, from_north = coefficients
    for _ in range(SUB):
        flux_east = from_here * content + from_east * rolled(content, -1, 1)
        flux_north = from_row * content + from_north * rolled(content, -1, 0)
        content = content - (
            (flux_east - rolled(flux_east, 1, 1)) + (flux_north - rolled(flux_north, 1, 0))
        )
    return content


def slots_of(levels, width):
    per_tile = width // SLOT
    tiles = -(-levels // per_tile)
    return [[(s, t * per_tile + s) for s in range(min(per_tile, levels - t * per_tile))] for t in range(tiles)]


def window_tile(plane_of, slots, offset):
    tile = None
    for slot, level in slots:
        moved = rolled(plane_of(level), SLOT * slot + offset, 1)
        tile = moved if tile is None else jnp.where(lanes_of(moved) >= SLOT * slot, moved, tile)
    return tile


def plane_readers(tracer_ref, east_ref, north_ref, mixing_ref, wet_of):
    tracers = [functools.partial(lambda i, k: tracer_ref[i, k], i) for i in range(tracer_ref.shape[0])]
    return tracers + [lambda k: east_ref[k], lambda k: north_ref[k], lambda k: mixing_ref[k], wet_of]


def pack_kernel(tracer, east, north, mixing, mask, bottom, east_tiles, to_far, to_near):
    levels, _, width = mask.shape
    first_level = lax.axis_index("gz") * levels
    even = lax.axis_index("gx") % 2 == 0
    wet_of = lambda k: wetness(mask, bottom[...], k, first_level)
    readers = plane_readers(tracer, east, north, mixing, wet_of)
    for t, slots in enumerate(slots_of(levels, width)):
        tiles = [window_tile(reader, slots, 2 * SUB) for reader in readers]
        for j, tile in enumerate(tiles):
            east_tiles[j, t] = tile
        for g in range(to_far.shape[0]):
            east_part = west_part = None
            for q in range(GROUP):
                if g * GROUP + q >= len(tiles):
                    break
                tile = tiles[g * GROUP + q]
                e = rolled(tile, SUB * (q - 1), 1)
                w = rolled(tile, SUB * (q - 2), 1)
                if q == 0:
                    east_part, west_part = e, w
                else:
                    inside = lax.rem(lanes_of(tile), SLOT) >= SUB * q
                    east_part = jnp.where(inside, e, east_part)
                    west_part = jnp.where(inside, w, west_part)
            to_far[g, t] = jnp.where(even, west_part, east_part)
            to_near[g, t] = jnp.where(even, east_part, west_part)


def interior_kernel(
    tracer, east, north, vertical, mixing, mixing_vertical, mask, bottom,
    west_tiles, lateral, down, up, from_first, from_last, pivots, ratios, carries, rims,
):
    levels, _, width = mask.shape
    first_level = lax.axis_index("gz") * levels
    wet_of = lambda k: wetness(mask, bottom[...], k, first_level)
    wet_first = wet = wet_of(0)
    couplings = []
    rest = jnp.ones_like(wet)
    for k in range(levels - 1):
        wet_below = wet_of(k + 1)
        both = wet * wet_below
        coupling = mixing_vertical[k] * both
        speed = vertical[k] * both
        down[k] = jnp.maximum(speed, 0.0)
        up[k] = jnp.minimum(speed, 0.0)
        inverse = 1.0 / (rest + coupling)
        pivots[k] = inverse
        ratio = coupling * inverse
        ratios[k] = ratio
        carries[k] = coupling
        rest = 1.0 + ratio * rest
        couplings.append(coupling)
        wet = wet_below
    weight = 1.0 / rest
    pivots[levels - 1] = weight
    from_last[levels - 1] = weight
    last_own = weight
    for k in range(levels - 2, -1, -1):
        weight = ratios[k] * weight
        from_last[k] = weight
    across = weight
    rest = jnp.ones_like(wet)
    upward = []
    for k in range(levels - 2, -1, -1):
        ratio = couplings[k] / (rest + couplings[k])
        upward.append(ratio)
        rest = 1.0 + ratio * rest
    weight = 1.0 / rest
    from_first[0] = weight
    for k in range(levels - 1):
        weight = upward[levels - 2 - k] * weight
        from_first[k + 1] = weight
    link = wet * mixing_vertical[levels - 1]
    speed = wet * vertical[levels - 1]
    scale = 1.0 / (1.0 + link * last_own)
    rims[0] = link * scale
    rims[1] = jnp.maximum(speed, 0.0) * scale
    rims[2] = jnp.minimum(speed, 0.0) * scale
    rims[3] = wet_first * rest
    rims[4] = across
    for k in range(levels):
        coefficients = lateral_coefficients(east[k], north[k], mixing[k], wet_of(k))
        for i in range(tracer.shape[0]):
            lateral[i, k] = lateral_substeps(tracer[i, k], coefficients)
    readers = plane_readers(tracer, east, north, mixing, wet_of)
    for t, slots in enumerate(slots_of(levels, width)):
        for j, reader in enumerate(readers):
            west_tiles[j, t] = window_tile(reader, slots, SUB)


def rim_kernel(
    east_tiles, west_tiles, far, near, lateral, down, up, from_first, from_last, rims,
    forcing, message,
):
    tracers, levels, _, width = lateral.shape
    even = lax.axis_index("gx") % 2 == 0
    edges = []
    for t, slots in enumerate(slots_of(levels, width)):
        lane = lax.rem(lanes_of(bottom_like(lateral)), SLOT)
        from_west = [jnp.where(even, far[g, t], near[g, t]) for g in range(far.shape[0])]
        from_east = [jnp.where(even, near[g, t], far[g, t]) for g in range(far.shape[0])]
        west, east = [], []
        for j in range(east_tiles.shape[0]):
            g, q = divmod(j, GROUP)
            west.append(jnp.where(lane < SUB, rolled(from_west[g], -SUB * q, 1), west_tiles[j, t]))
            east.append(
                jnp.where(lane >= 2 * SUB, rolled(from_east[g], SUB * (2 - q), 1), east_tiles[j, t])
            )
        west_steps = lateral_coefficients(*west[tracers:])
        east_steps = lateral_coefficients(*east[tracers:])
        done = []
        for i in range(tracers):
            west_done = lateral_substeps(west[i], west_steps)
            east_done = lateral_substeps(east[i], east_steps)
            done.append(jnp.where(lane < SUB, rolled(east_done, -SUB, 1), west_done))
        edges.append(done)
    per_tile = width // SLOT
    for i in range(tracers):
        above = flux_above = None
        first_sum = last_sum = None
        for k in range(levels + 1):
            if k < levels:
                t, s = divmod(k, per_tile)
                edge = rolled(edges[t][i], width - SUB - SLOT * s, 1)
                lane = lanes_of(edge)
                here = jnp.where((lane < SUB) | (lane >= width - SUB), edge, lateral[i, k])
            if k == 0:
                first = above = here
                continue
            if k < levels:
                flux = down[k - 1] * here + up[k - 1] * above
                value = above + (flux if k == 1 else flux - flux_above)
                flux_above = flux
            else:
                value = above - flux_above
            forcing[i, k - 1] = value
            a = from_first[k - 1] * value
            b = from_last[k - 1] * value
            first_sum = a if k == 1 else first_sum + a
            last_sum = b if k == 1 else last_sum + b
            above = here
        message[i] = rims[0] * last_sum - rims[2] * above
        message[tracers + 2 + i] = rims[3] * first_sum
        message[2 * tracers + 2 + i] = rims[3] * first
    message[tracers] = rims[0]
    message[tracers + 1] = rims[1]
    message[3 * tracers + 2] = rims[3]
    message[3 * tracers + 3] = rims[4]


def bottom_like(ref):
    return jnp.zeros(ref.shape[-2:], jnp.float32)


def block_kernel(forcing, pivots, ratios, carries, solved):
    tracers, levels = forcing.shape[:2]
    for i in range(tracers):
        value = forcing[i, 0] * pivots[0]
        values = [value]
        for k in range(1, levels):
            value = (forcing[i, k] + carries[k - 1] * value) * pivots[k]
            values.append(value)
        solved[i, levels - 1] = value
        for k in range(levels - 2, -1, -1):
            value = values[k] + ratios[k] * value
            solved[i, k] = value


def interface(upper, lower, tracers):
    heads, alpha, beta = upper[:tracers], upper[tracers], upper[tracers + 1]
    sums, rims, admit = lower[:tracers], lower[tracers : 2 * tracers], lower[2 * tracers]
    inverse = jnp.where(admit > 0.0, 1.0 / (admit + alpha), 0.0)
    flux = [(alpha * s + beta * r - admit * h) * inverse for s, r, h in zip(sums, rims, heads)]
    return flux, admit * alpha * inverse


def pair_kernel(own, other, merged, kept):
    tracers = kept.shape[0] - 1
    z = lax.axis_index("gz")
    lower_here = z % 2 == 1
    lower_pair = z >= 2
    upper, lower = [], []
    count = own.shape[0]
    for j in range(count):
        upper.append(jnp.where(lower_here, other[j], own[j]))
        lower.append(jnp.where(lower_here, own[j], other[j]))
    n = tracers + 2
    flux, gain = interface(upper[:n], lower[n:-1], tracers)
    across = jnp.where(lower_pair, upper[-1], lower[-1])
    gain = gain * across
    for i in range(tracers):
        kept[i] = flux[i]
    kept[tracers] = gain
    factor = across * jnp.where(lower_pair, upper[-2], lower[tracers])
    scale = 1.0 / (1.0 - factor * gain)
    for i in range(tracers):
        head = jnp.where(lower_pair, upper[n + i] + factor * flux[i], lower[i] - factor * flux[i])
        merged[i] = head * scale
    for i in range(tracers + 1):
        merged[tracers + i] = scale * (
            jnp.where(lower_pair, upper[n + tracers + i], lower[tracers + i] if i < 2 else 0.0)
        )


def final_kernel(own, other, kept, solved, from_first, from_last, out):
    tracers, levels = solved.shape[:2]
    z = lax.axis_index("gz")
    lower_pair = z >= 2
    upper = [jnp.where(lower_pair, other[j], own[j]) for j in range(own.shape[0])]
    lower = [jnp.where(lower_pair, own[j], other[j]) for j in range(own.shape[0])]
    middle, _ = interface(upper[: tracers + 2], lower, tracers)
    for i in range(tracers):
        near = kept[i] + kept[tracers] * middle[i]
        top = jnp.where(z == 0, 0.0, jnp.where(z == 2, middle[i], near))
        low = jnp.where(z == 3, 0.0, jnp.where(z == 1, middle[i], near))
        for k in range(levels):
            out[i, k] = solved[i, k] - top * from_first[k] + low * from_last[k]


def local(
    tracer, east_flow, north_flow, vertical_flow, mixing_lateral, mixing_vertical, sea_mask, bottom
):
    tracers, levels, rows, width = tracer.shape
    arrays = tracers + 4
    tiles = len(slots_of(levels, width))
    groups = -(-arrays // GROUP)
    plane = (rows, width)
    block = (levels, rows, width)
    ring = lax.axis_size("gx")
    cells = levels * rows * width
    near_pairs = [(i, i ^ 1) for i in range(ring)]
    far_pairs = [(i, (i + 1) % ring if i % 2 else (i - 1) % ring) for i in range(ring)]

    east_tiles, to_far, to_near = call(
        pack_kernel,
        [(arrays, tiles) + plane, (groups, tiles) + plane, (groups, tiles) + plane],
        10 * cells,
        tracer, east_flow, north_flow, mixing_lateral, sea_mask, bottom,
    )
    far = lax.ppermute(to_far, "gx", far_pairs)
    near = lax.ppermute(to_near, "gx", near_pairs)
    west_tiles, lateral, down, up, from_first, from_last, pivots, ratios, carries, rims = call(
        interior_kernel,
        [(arrays, tiles) + plane, tracer.shape] + [block] * 7 + [(5,) + plane],
        150 * cells,
        tracer, east_flow, north_flow, vertical_flow, mixing_lateral, mixing_vertical, sea_mask, bottom,
    )
    forcing, message = call(
        rim_kernel,
        [tracer.shape, (3 * tracers + 4,) + plane],
        40 * cells,
        east_tiles, west_tiles, far, near, lateral, down, up, from_first, from_last, rims,
    )
    other = lax.ppermute(message, "gz", [(i, i ^ 1) for i in range(4)])
    (solved,) = call(block_kernel, [tracer.shape], 30 * cells, forcing, pivots, ratios, carries)
    merged, kept = call(
        pair_kernel, [(2 * tracers + 1,) + plane, (tracers + 1,) + plane], cells, message, other
    )
    beyond = lax.ppermute(merged, "gz", [(i, i ^ 2) for i in range(4)])
    (result,) = call(
        final_kernel, [tracer.shape], 10 * cells, merged, beyond, kept, solved, from_first, from_last
    )
    return result


def solution(mesh):
    assert mesh.shape["gz"] == 4 and mesh.shape["gx"] % 2 == 0
    return jax.shard_map(
        local,
        mesh=mesh,
        in_specs=(
            P(None, "gz", None, "gx"),
            P("gz", None, "gx"),
            P("gz", None, "gx"),
            P("gz", None, "gx"),
            P("gz", None, "gx"),
            P("gz", None, "gx"),
            P("gz", None, "gx"),
            P(None, "gx"),
        ),
        out_specs=P(None, "gz", None, "gx"),
        check_vma=False,
    )
```

time: 125 us -> 32.5 us (0.26)
  waiting for transfers between devices: 39.8 us -> 5.63 us
  local copies, waits for them, and re-layouts: 27.4 us -> 5.42 us
  starting transfers between devices: 29.4 us -> 7.7 us
  blocking collectives: 13.7 us -> 0 us
  Pallas kernels: 0 us -> 13.4 us
  other arithmetic: 13.4 us -> 0 us
    ppermute x10 -> x4, waiting for transfers between devices: 29.4 us -> 5.63 us  [the longest x1 3.27 us: local(): other = lax.ppermute(message, 'gz', [(i, i ^ 1) for i in range(4)])]
    all_to_all x1 -> x0, blocking collectives: 13.7 us -> none  [settle_mix(): lax.all_to_all(mixed_out, 'gz', split_axis=1, concat_axis=2, tiled=True)]
    pallas_call x0 -> x6, Pallas kernels: none -> 13.4 us  [call(): pl.pallas_call(kernel, out_shape=outs, in_specs=[VMEM] * len(operands), o...]
    all_to_all x2 -> x0, starting transfers between devices: 11.6 us -> none  [the longest x1 5.93 us: local(): lax.all_to_all(tracers_now, 'gz', split_axis=2, concat_axis=1, tiled=True)]
    all_to_all x2 -> x0, waiting for transfers between devices: 10.4 us -> none  [the longest x1 10.4 us: local(): lax.all_to_all(tracers_now, 'gz', split_axis=2, concat_axis=1, tiled=True)]
    ppermute x10 -> x4, starting transfers between devices: 17.9 us -> 7.7 us  [the longest x1 3.4 us: local(): far = lax.ppermute(to_far, 'gx', far_pairs)]
    another operation x5 -> x0, local copies, waits for them, and re-layouts: 5.59 us -> none  [the longest x2 2.9 us: local(): jnp.stack([east_flow, mixing_lateral, wet_cells])]
    unnamed x60 -> x16, local copies, waits for them, and re-layouts: 11 us -> 5.42 us
  transfers between devices with their start and end apart: 12 -> 4, of which waited for: 6 -> 2; matrix products, arithmetic and copies ran while one was open for 23% -> 0% of each run, Pallas kernels for 0% -> 35%
where the time goes in v1:
time: 32.5 us; the launch traced here: 32.2 us
  Pallas kernels  13.4 us (41%)
  starting transfers between devices  7.7 us (24%)
  waiting for transfers between devices  5.63 us (17%)
  local copies, waits for them, and re-layouts  5.42 us (17%)
    pallas_call x6, Pallas kernels, call(): pl.pallas_call(kernel, out_shape=outs, in_specs=[VMEM] * len(operands), o...  13.4 us
    unnamed x16, local copies, waits for them, and re-layouts  5.42 us
    ppermute x1, starting transfers between devices, local(): far = lax.ppermute(to_far, 'gx', far_pairs)  3.4 us
    ppermute x1, waiting for transfers between devices, local(): other = lax.ppermute(message, 'gz', [(i, i ^ 1) for i in range(4)])  3.27 us
    ppermute x1, starting transfers between devices, local(): beyond = lax.ppermute(merged, 'gz', [(i, i ^ 2) for i in range(4)])  2.65 us
    ppermute x1, waiting for transfers between devices, local(): beyond = lax.ppermute(merged, 'gz', [(i, i ^ 2) for i in range(4)])  2.35 us
    ppermute x1, starting transfers between devices, local(): other = lax.ppermute(message, 'gz', [(i, i ^ 1) for i in range(4)])  1.64 us
  transfers between devices with their start and end apart: 4, of which 2 were waited for; matrix products, arithmetic and copies ran while one was open for 0% of the time, Pallas kernels for 35%

profile of v1, /device:TPU:0, one launch (start us, length us, event | category | flops | bytes accessed | tf_op | source)
XLA Modules:
  0.0 32.2 jit_solution(15633743458866078879)
XLA Ops:
  0.0 0.0 copy-start
  0.0 1.0 %copy-done = f32[2,25,16,128]{3,2,1,0:T(8,128)S(1)} copy-done((f32[2,25,16,128]{3,2,1,0:T(8,128)S(1)}, f32[2,25,16,128]{3,2,1,0:T(8,128)}, u32[]{:S(2)}) %copy-start) | copy-done | bytes 409624
  1.0 0.0 copy-start.1
  1.0 0.9 %copy-done.1 = f32[25,16,128]{2,1,0:T(8,128)S(1)} copy-done((f32[25,16,128]{2,1,0:T(8,128)S(1)}, f32[25,16,128]{2,1,0:T(8,128)}, u32[]{:S(2)}) %copy-start.1) | copy-done | bytes 204824
  1.9 0.0 copy-start.2
  1.9 0.9 %copy-done.2 = f32[25,16,128]{2,1,0:T(8,128)S(1)} copy-done((f32[25,16,128]{2,1,0:T(8,128)S(1)}, f32[25,16,128]{2,1,0:T(8,128)}, u32[]{:S(2)}) %copy-start.2) | copy-done | bytes 204824
  2.9 0.9 %copy-done.3 = f32[25,16,128]{2,1,0:T(8,128)S(1)} copy-done((f32[25,16,128]{2,1,0:T(8,128)S(1)}, f32[25,16,128]{2,1,0:T(8,128)}, u32[]{:S(2)}) %copy-start.3) | copy-done | bytes 204824
  3.8 0.9 %copy-done.4 = s32[25,16,128]{2,1,0:T(8,128)S(1)} copy-done((s32[25,16,128]{2,1,0:T(8,128)S(1)}, s32[25,16,128]{2,1,0:T(8,128)}, u32[]{:S(2)}) %copy-start.4) | copy-done | bytes 204824
  4.7 0.7 %copy-done.7 = s32[16,128]{1,0:T(8,128)S(1)} copy-done((s32[16,128]{1,0:T(8,128)S(1)}, s32[16,128]{1,0:T(8,128)}, u32[]{:S(2)}) %copy-start.7) | copy-done | bytes 8216
  5.4 0.5 %shard_map.82 = (f32[6,2,16,128]{3,2,1,0:T(8,128)S(1)}, f32[2,2,16,128]{3,2,1,0:T(8,128)S(1)}, f32[2,2,16,128]{3,2,1,0:T(8,128)S(1)}) custom-call(f32[2,25,16,128]{3,2,1,0:T(8,128)S(1)} %copy-done, f32[25,16,128]{2,1,0:T(8,128)S(1)} %copy-done.1, f32[25,16,128]{2,1,0:T(8,128)S(1)} %copy-done.2, f32[25,16,128]{2,1,0:T(8,128)S(1)} %copy-done.3, ...), custom_call_target="tpu_custom_call" | custom-call | flops 512000 | bytes 1400832 | tf_op jit(solution)/shard_map/pallas_call | solution.py:20
  5.9 3.4 %collective-permute-start = (f32[2,2,16,128]{3,2,1,0:T(8,128)S(1)}, f32[2,2,16,128]{3,2,1,0:T(8,128)S(1)}, u32[]{:S(2)}, u32[]{:S(2)}) collective-permute-start(f32[2,2,16,128]{3,2,1,0:T(8,128)S(1)} %get-tuple-element.24), channel_id=1, source_target_pairs={{0,28},{4,8},{8,4},{12,16},{16,12},{20,24},{24,20},{28,0},{1,29},{... | collective-permute-start | bytes 98312 | tf_op jit(solution)/shard_map/ppermute | solution.py:326
  9.3 0.0 collective-permute-start.1
  9.3 0.0 copy-done.5
  9.3 0.0 copy-done.6
  9.3 11.0 %shard_map.83 = (f32[6,2,16,128]{3,2,1,0:T(8,128)S(1)}, f32[2,25,16,128]{3,2,1,0:T(8,128)S(1)}, f32[25,16,128]{2,1,0:T(8,128)S(1)}, f32[25,16,128]{2,1,0:T(8,128...) custom-call(f32[2,25,16,128]{3,2,1,0:T(8,128)S(1)} %copy-done, ...), custom_call_target="tpu_custom_call" | custom-call | flops 7680000 | bytes 3629056 | tf_op jit(solution)/shard_map/pallas_call | solution.py:20
  20.3 0.0 collective-permute-done.far
  20.4 0.0 collective-permute-done.1.near
  20.4 0.8 %shard_map.84 = (f32[2,25,16,128]{3,2,1,0:T(8,128)S(1)}, f32[10,16,128]{2,1,0:T(8,128)S(1)}) custom-call(f32[6,2,16,128]{3,2,1,0:T(8,128)S(1)} %get-tuple-element.22.east_tiles, f32[6,2,16,128]{3,2,1,0:T(8,128)S(1)} %get-tuple-element.23.west_tiles, f32[2,2,16,128]{3,2,1,0:T(8,128)S(1)} %collective-permute-done.far, ...), custom_call_target="tpu_custom_call" | custom-call | flops 2048000 | bytes 2023424 | tf_op jit(solution)/shard_map/pallas_call | solution.py:20
  21.2 1.6 %collective-permute-start.2 = (f32[10,16,128]{2,1,0:T(8,128)S(1)}, f32[10,16,128]{2,1,0:T(8,128)S(1)}, u32[]{:S(2)}, u32[]{:S(2)}) collective-permute-start(f32[10,16,128]{2,1,0:T(8,128)S(1)} %get-tuple-element.32.own), channel_id=1, source_target_pairs={{0,1},{1,0},{2,3},{3,2},{4,5},{5,4},{6,7},{7,6},{8,9},{9,8},{10,11... | collective-permute-start | bytes 245768 | tf_op jit(solution)/shard_map/ppermute | solution.py:340
  22.8 3.3 %collective-permute-done.2.other = f32[10,16,128]{2,1,0:T(8,128)S(1)} collective-permute-done((f32[10,16,128]{2,1,0:T(8,128)S(1)}, f32[10,16,128]{2,1,0:T(8,128)S(1)}, u32[]{:S(2)}, u32[]{:S(2)}) %collective-permute-start.2) | collective-permute-done | bytes 81952 | tf_op jit(solution)/shard_map/ppermute | solution.py:340
  26.1 2.7 %collective-permute-start.3 = (f32[5,16,128]{2,1,0:T(8,128)S(1)}, f32[5,16,128]{2,1,0:T(8,128)S(1)}, u32[]{:S(2)}, u32[]{:S(2)}) collective-permute-start(f32[5,16,128]{2,1,0:T(8,128)S(1)} %get-tuple-element.33.own), channel_id=1, source_target_pairs={{0,2},{1,3},{2,0},{3,1},{4,6},{5,7},{6,4},{7,5},{8,10},{9,11},{10,... | collective-permute-start | bytes 122888 | tf_op jit(solution)/shard_map/ppermute | solution.py:345
  28.8 0.2 shard_map.86.solved
  29.0 2.4 %collective-permute-done.3.other = f32[5,16,128]{2,1,0:T(8,128)S(1)} collective-permute-done((f32[5,16,128]{2,1,0:T(8,128)S(1)}, f32[5,16,128]{2,1,0:T(8,128)S(1)}, u32[]{:S(2)}, u32[]{:S(2)}) %collective-permute-start.3) | collective-permute-done | bytes 40992 | tf_op jit(solution)/shard_map/ppermute | solution.py:345
  31.3 0.9 %shard_map.87 = f32[2,25,16,128]{3,2,1,0:T(8,128)} custom-call(f32[5,16,128]{2,1,0:T(8,128)S(1)} %get-tuple-element.33.own, f32[5,16,128]{2,1,0:T(8,128)S(1)} %collective-permute-done.3.other, f32[3,16,128]{2,1,0:T(8,128)S(1)} %get-tuple-element.34.kept, f32[2,25,16,128]{3,2,1,0:T(8,128)S(1)} %shard_map.86.solved, ...), custom_call_target="tpu_custom_call" | custom-call | flops 512000 | bytes 1335296 | tf_op jit(solution)/shard_map/pallas_call | solution.py:20
  (6 shorter events, 0.0 us)
Async XLA Ops:
  0.0 1.0 %copy-start = (f32[2,25,16,128]{3,2,1,0:T(8,128)S(1)}, f32[2,25,16,128]{3,2,1,0:T(8,128)}, u32[]{:S(2)}) copy-start(f32[2,25,16,128]{3,2,1,0:T(8,128)} %tracer.3) | copy-start | bytes 1228804
  1.0 0.9 %copy-start.1 = (f32[25,16,128]{2,1,0:T(8,128)S(1)}, f32[25,16,128]{2,1,0:T(8,128)}, u32[]{:S(2)}) copy-start(f32[25,16,128]{2,1,0:T(8,128)} %east.3) | copy-start | bytes 614404
  1.9 0.9 %copy-start.2 = (f32[25,16,128]{2,1,0:T(8,128)S(1)}, f32[25,16,128]{2,1,0:T(8,128)}, u32[]{:S(2)}) copy-start(f32[25,16,128]{2,1,0:T(8,128)} %north.3) | copy-start | bytes 614404
  2.9 0.9 %copy-start.3 = (f32[25,16,128]{2,1,0:T(8,128)S(1)}, f32[25,16,128]{2,1,0:T(8,128)}, u32[]{:S(2)}) copy-start(f32[25,16,128]{2,1,0:T(8,128)} %mixing.3) | copy-start | bytes 614404
  3.8 0.9 %copy-start.4 = (s32[25,16,128]{2,1,0:T(8,128)S(1)}, s32[25,16,128]{2,1,0:T(8,128)}, u32[]{:S(2)}) copy-start(s32[25,16,128]{2,1,0:T(8,128)} %mask.3) | copy-start | bytes 614404
  4.7 0.7 %copy-start.7 = (s32[16,128]{1,0:T(8,128)S(1)}, s32[16,128]{1,0:T(8,128)}, u32[]{:S(2)}) copy-start(s32[16,128]{1,0:T(8,128)} %bottom.3) | copy-start | bytes 24580
  5.4 3.9 %copy-start.5 = (f32[25,16,128]{2,1,0:T(8,128)S(1)}, f32[25,16,128]{2,1,0:T(8,128)}, u32[]{:S(2)}) copy-start(f32[25,16,128]{2,1,0:T(8,128)} %vertical.1) | copy-start | bytes 614404
  5.4 3.9 %copy-start.6 = (f32[25,16,128]{2,1,0:T(8,128)S(1)}, f32[25,16,128]{2,1,0:T(8,128)}, u32[]{:S(2)}) copy-start(f32[25,16,128]{2,1,0:T(8,128)} %mixing_vertical.1) | copy-start | bytes 614404
  5.9 14.4 %collective-permute-start = (f32[2,2,16,128]{3,2,1,0:T(8,128)S(1)}, f32[2,2,16,128]{3,2,1,0:T(8,128)S(1)}, u32[]{:S(2)}, u32[]{:S(2)}) collective-permute-start(f32[2,2,16,128]{3,2,1,0:T(8,128)S(1)} %get-tuple-element.24), channel_id=1, source_target_pairs={{0,28},{4,8},{8,4},{12,16},{16,12},{20,24},{24,20},{28,0},{1,29},{... | collective-permute-start | bytes 98312 | tf_op jit(solution)/shard_map/ppermute | solution.py:326
  9.3 11.0 %collective-permute-start.1 = (f32[2,2,16,128]{3,2,1,0:T(8,128)S(1)}, f32[2,2,16,128]{3,2,1,0:T(8,128)S(1)}, u32[]{:S(2)}, u32[]{:S(2)}) collective-permute-start(f32[2,2,16,128]{3,2,1,0:T(8,128)S(1)} %get-tuple-element.25), channel_id=1, source_target_pairs={{0,4},{4,0},{8,12},{12,8},{16,20},{20,16},{24,28},{28,24},{1,5},{5... | collective-permute-start | bytes 98312 | tf_op jit(solution)/shard_map/ppermute | solution.py:327
  21.2 4.9 %collective-permute-start.2 = (f32[10,16,128]{2,1,0:T(8,128)S(1)}, f32[10,16,128]{2,1,0:T(8,128)S(1)}, u32[]{:S(2)}, u32[]{:S(2)}) collective-permute-start(f32[10,16,128]{2,1,0:T(8,128)S(1)} %get-tuple-element.32.own), channel_id=1, source_target_pairs={{0,1},{1,0},{2,3},{3,2},{4,5},{5,4},{6,7},{7,6},{8,9},{9,8},{10,11... | collective-permute-start | bytes 245768 | tf_op jit(solution)/shard_map/ppermute | solution.py:340
  26.1 5.2 %collective-permute-start.3 = (f32[5,16,128]{2,1,0:T(8,128)S(1)}, f32[5,16,128]{2,1,0:T(8,128)S(1)}, u32[]{:S(2)}, u32[]{:S(2)}) collective-permute-start(f32[5,16,128]{2,1,0:T(8,128)S(1)} %get-tuple-element.33.own), channel_id=1, source_target_pairs={{0,2},{1,3},{2,0},{3,1},{4,6},{5,7},{6,4},{7,5},{8,10},{9,11},{10,... | collective-permute-start | bytes 122888 | tf_op jit(solution)/shard_map/ppermute | solution.py:345

commit v2 on v1

v2 whole, which is shorter than its diff:
```python
import jax
import jax.numpy as jnp
from jax import lax
from jax.experimental import pallas as pl
from jax.experimental.pallas import tpu as pltpu
from jax.sharding import PartitionSpec as P

SUB = 3
SLOT = 3 * SUB
GROUP = SLOT // SUB

VMEM = pl.BlockSpec(memory_space=pltpu.VMEM)
HBM = pl.BlockSpec(memory_space=pltpu.HBM)


def call(kernel, shapes, flops, *operands, in_specs=None, out_specs=None, scratch=()):
    outs = [jax.ShapeDtypeStruct(s, jnp.float32) for s in shapes]
    if in_specs is not None:
        operands = [pltpu.with_memory_space_constraint(x, pltpu.HBM) if p is HBM else x for x, p in zip(operands, in_specs)]
    size = sum(o.size * o.dtype.itemsize for o in (*operands, *outs))
    return pl.pallas_call(
        kernel,
        out_shape=outs,
        in_specs=in_specs or [VMEM] * len(operands),
        out_specs=out_specs or [VMEM] * len(outs),
        scratch_shapes=list(scratch),
        compiler_params=pltpu.CompilerParams(vmem_limit_bytes=24 * 2**20),
        cost_estimate=pl.CostEstimate(flops=flops, bytes_accessed=size, transcendentals=0),
    )(*operands)


def rolled(plane, shift, axis):
    return pltpu.roll(plane, shift % plane.shape[axis], axis)


def lanes_of(plane):
    return lax.broadcasted_iota(jnp.int32, plane.shape, 1)


def lateral_coefficients(east, north, mixing, wet):
    rows = east.shape[0]
    open_east = wet * rolled(wet, -1, 1)
    mean_east = 0.5 * (mixing + rolled(mixing, -1, 1))
    row = lax.broadcasted_iota(jnp.int32, wet.shape, 0)
    open_north = jnp.where(row < rows - 1, wet * rolled(wet, -1, 0), 0.0)
    mean_north = 0.5 * (mixing + rolled(mixing, -1, 0))
    return (
        open_east * (jnp.maximum(east, 0.0) + mean_east),
        open_east * (jnp.minimum(east, 0.0) - mean_east),
        open_north * (jnp.maximum(north, 0.0) + mean_north),
        open_north * (jnp.minimum(north, 0.0) - mean_north),
    )


def lateral_substeps(planes, coefficients):
    for _ in range(SUB):
        east = {q: rolled(c, -1, 1) for q, c in planes.items()}
        flux_east = {q: coefficients[q[1]][0] * c + coefficients[q[1]][1] * east[q] for q, c in planes.items()}
        flux_west = {q: rolled(f, 1, 1) for q, f in flux_east.items()}
        flux_north = {
            q: coefficients[q[1]][2] * c + coefficients[q[1]][3] * rolled(c, -1, 0) for q, c in planes.items()
        }
        planes = {
            q: c - ((flux_east[q] - flux_west[q]) + (flux_north[q] - rolled(flux_north[q], 1, 0)))
            for q, c in planes.items()
        }
    return planes


def stencil(east, north, mixing, wet):
    rows = east.shape[0]
    wet_west, mixing_west, east_west = (rolled(x, 1, 1) for x in (wet, mixing, east))
    open_east = wet * rolled(wet, -1, 1)
    mean_east = 0.5 * (mixing + rolled(mixing, -1, 1))
    open_west = wet * wet_west
    mean_west = 0.5 * (mixing + mixing_west)
    row = lax.broadcasted_iota(jnp.int32, wet.shape, 0)
    open_north = jnp.where(row < rows - 1, wet * rolled(wet, -1, 0), 0.0)
    mean_north = 0.5 * (mixing + rolled(mixing, -1, 0))
    east_in = open_east * (mean_east - jnp.minimum(east, 0.0))
    east_out = open_east * (mean_east + jnp.maximum(east, 0.0))
    west_in = open_west * (mean_west + jnp.maximum(east_west, 0.0))
    west_out = open_west * (mean_west - jnp.minimum(east_west, 0.0))
    north_in = open_north * (mean_north - jnp.minimum(north, 0.0))
    north_out = open_north * (mean_north + jnp.maximum(north, 0.0))
    south_in = rolled(north_out, 1, 0)
    south_out = rolled(north_in, 1, 0)
    here = 1.0 - ((east_out + west_out) + (north_out + south_out))
    return here, east_in, west_in, north_in, south_in


def stencil_substeps(planes, weights):
    for _ in range(SUB):
        sides = {q: (rolled(c, -1, 1), rolled(c, 1, 1), rolled(c, -1, 0), rolled(c, 1, 0)) for q, c in planes.items()}
        planes = {
            q: (weights[q[1]][0] * c + weights[q[1]][3] * sides[q][2] + weights[q[1]][4] * sides[q][3])
            + (weights[q[1]][1] * sides[q][0] + weights[q[1]][2] * sides[q][1])
            for q, c in planes.items()
        }
    return planes


def slots_of(levels, width):
    per_tile = width // SLOT
    tiles = -(-levels // per_tile)
    return [[(s, t * per_tile + s) for s in range(min(per_tile, levels - t * per_tile))] for t in range(tiles)]


def window_tiles(plane_of, slots):
    moved = [(slot, rolled(plane_of(level), SLOT * slot + SUB, 1)) for slot, level in slots]
    lane = lanes_of(moved[0][1])
    tiles = []
    for ahead in (0, SUB):
        parts = moved
        while len(parts) > 1:
            pairs = [parts[n : n + 2] for n in range(0, len(parts), 2)]
            parts = [
                p[0] if len(p) == 1 else (p[0][0], jnp.where(lane >= SLOT * p[1][0] - ahead, p[1][1], p[0][1]))
                for p in pairs
            ]
        tiles.append(parts[0][1])
    return tiles[0], jnp.where(lane >= lane.shape[1] - SUB, moved[0][1], tiles[1])


def pack_group(tiles, first_columns):
    lane = lax.rem(lanes_of(tiles[0]), SLOT)
    packed = None
    for q, tile in enumerate(tiles):
        moved = jnp.where(first_columns, rolled(tile, SUB * (q - 1), 1), rolled(tile, SUB * q, 1))
        packed = moved if q == 0 else jnp.where(lane >= SUB * q, moved, packed)
    return packed


def pack_kernel(
    tracer_in, mixing_in, east_in, north_in, mask_in, bottom_in, vertical_in, mixing_vertical_in,
    tracer, mixing, east, north, wet, vertical, mixing_vertical, west_tiles, east_tiles, to_far, mask, bottom, sems,
):
    levels, _, width = mask.shape
    tracers = tracer.shape[0]
    pairs = [(bottom_in, bottom), (mask_in, mask), (mixing_in, mixing), (east_in, east), (north_in, north)]
    pairs += [(tracer_in.at[i], tracer.at[i]) for i in range(tracers)]
    pairs += [(vertical_in, vertical), (mixing_vertical_in, mixing_vertical)]
    copies = [pltpu.make_async_copy(source, target, sems.at[n]) for n, (source, target) in enumerate(pairs)]
    for copy in copies:
        copy.start()
    slots = slots_of(levels, width)
    even = lax.axis_index("gx") % 2 == 0
    for copy in copies[:4]:
        copy.wait()
    floor = bottom[...] - lax.axis_index("gz") * levels
    signed = []
    for k in range(levels):
        is_wet = (mask[k] > 0) & (k < floor)
        wet[k] = jnp.where(is_wet, 1.0, 0.0)
        signed.append(jnp.where(is_wet, mixing[k], -mixing[k]))
    found = {}

    def find(j, t, pair):
        found[j, t] = pair[0]
        west_tiles[j, t], east_tiles[j, t] = pair

    for t, part in enumerate(slots):
        both = window_tiles(lambda k: signed[k], part)
        find(tracers, t, [jnp.abs(b) for b in both])
        find(tracers + 1, t, [jnp.where(b > 0.0, 1.0, 0.0) for b in both])
        find(tracers + 2, t, window_tiles(lambda k: east[k], part))
    for copy in copies[4:-2]:
        copy.wait()
    for t, part in enumerate(slots):
        for i in range(tracers):
            find(i, t, window_tiles(lambda k: tracer[i, k], part))
        find(tracers + 3, t, window_tiles(lambda k: north[k], part))
    for t in range(len(slots)):
        for g in range(to_far.shape[0]):
            to_far[g, t] = pack_group([found[g * GROUP + q, t] for q in range(GROUP)], even)
    for copy in copies[-2:]:
        copy.wait()


def side_kernel(
    wet, vertical, mixing_vertical, west_tiles,
    to_near, down, up, from_first, from_last, pivots, ratios, couplings, weights, rims,
):
    odd = lax.axis_index("gx") % 2 == 1
    for g, t in [(g, t) for g in range(to_near.shape[0]) for t in range(to_near.shape[1])]:
        to_near[g, t] = pack_group([west_tiles[g * GROUP + q, t] for q in range(GROUP)], odd)
    vertical_statics(
        wet, vertical, mixing_vertical, down, up, from_first, from_last, pivots, ratios, couplings, weights, rims
    )


def interior_kernel(tracer, mixing, east, north, wet, weights, lateral, sums):
    levels = wet.shape[0]
    tracers = tracer.shape[0]
    coefficients = {k: lateral_coefficients(east[k], north[k], mixing[k], wet[k]) for k in range(levels)}
    planes = {(i, k): tracer[i, k] for k in range(levels) for i in range(tracers)}
    planes = lateral_substeps(planes, coefficients)
    for i, k in planes:
        lateral[i, k] = planes[i, k]
    for i in range(tracers):
        for n in range(2):
            sums[n * tracers + i] = total([weights[n, k] * planes[i, k] for k in range(levels)])


def vertical_statics(
    wet_ref, vertical, mixing_vertical, down, up, from_first, from_last, pivots, ratios, couplings, weights, rims
):
    levels = wet_ref.shape[0]
    wet = [wet_ref[k] for k in range(levels)]
    both = [wet[k] * wet[k + 1] for k in range(levels - 1)]
    speeds = [vertical[k] * both[k] for k in range(levels - 1)]
    links = [mixing_vertical[k] * both[k] for k in range(levels - 1)]
    one = jnp.ones_like(wet[0])
    top_p = top_q = low_p = low_q = one
    pivot, ratio, upward = [None] * levels, [None] * levels, [None] * levels
    for k in range(levels - 1):
        next_q = top_p + links[k] * top_q
        next_p = next_q + links[k] * top_p
        inverse = 1.0 / next_q
        pivot[k] = top_q * inverse
        ratio[k] = links[k] * pivot[k]
        top_p, top_q = next_p, next_q
        m = levels - 2 - k
        next_q = low_p + links[m] * low_q
        next_p = next_q + links[m] * low_p
        low_inverse = 1.0 / next_q
        upward[m] = links[m] * low_q * low_inverse
        low_p, low_q = next_p, next_q
        if k % 6 == 5:
            top_p, top_q = top_p * inverse, one
            low_p, low_q = low_p * low_inverse, one
    last, first = [None] * levels, [None] * levels
    last[-1] = pivot[-1] = top_q / top_p
    first[0] = low_q / low_p
    for k in range(levels - 1):
        m = levels - 2 - k
        last[m] = ratio[m] * last[m + 1]
        first[k + 1] = upward[k] * first[k]
    link = wet[-1] * mixing_vertical[levels - 1]
    speed = wet[-1] * vertical[levels - 1]
    scale = 1.0 / (1.0 + link * last[-1])
    rim = [link * scale, jnp.maximum(speed, 0.0) * scale, jnp.minimum(speed, 0.0) * scale]
    rim += [wet[0] * low_p / low_q, last[0]]
    for k in range(levels):
        pivots[k], from_first[k], from_last[k] = pivot[k], first[k], last[k]
    for k in range(levels - 1):
        ratios[k], couplings[k] = ratio[k], links[k]
        down[k], up[k] = jnp.maximum(speeds[k], 0.0), jnp.minimum(speeds[k], 0.0)
    for n, column in enumerate((first, last)):
        for k in range(levels):
            weight = column[k]
            if k < levels - 1:
                weight = weight + jnp.minimum(speeds[k], 0.0) * (column[k] - column[k + 1])
            if k > 0:
                weight = weight + jnp.maximum(speeds[k - 1], 0.0) * (column[k - 1] - column[k])
            weights[n, k] = weight
    for n, value in enumerate(rim):
        rims[n] = value


def rim_kernel(west_tiles, east_tiles, far, near, lateral, weights, sums, rims, edges, message):
    tracers, levels, _, width = lateral.shape
    even = lax.axis_index("gx") % 2 == 0
    slots = slots_of(levels, width)
    arrays, tiles = east_tiles.shape[:2]
    lanes = lanes_of(rims[0])
    lane = lax.rem(lanes, SLOT)
    windows = {}
    for t in range(tiles):
        from_west = [jnp.where(even, far[g, t], near[g, t]) for g in range(far.shape[0])]
        from_east = [jnp.where(even, near[g, t], far[g, t]) for g in range(far.shape[0])]
        for j in range(arrays):
            g, q = divmod(j, GROUP)
            windows[j, t, 0] = jnp.where(lane < SUB, rolled(from_west[g], -SUB * q, 1), west_tiles[j, t])
            windows[j, t, 1] = jnp.where(
                (lane >= SUB) & (lane < 2 * SUB), rolled(from_east[g], SUB * (1 - q), 1), east_tiles[j, t]
            )
    places = [(t, side) for t in range(tiles) for side in range(2)]
    stencils = {p: stencil(*(windows[(tracers + j,) + p] for j in (2, 3, 0, 1))) for p in places}
    done = stencil_substeps({(i, p): windows[(i,) + p] for p in places for i in range(tracers)}, stencils)
    edge = {
        (i, t): jnp.where(lane < SUB, done[i, (t, 1)], done[i, (t, 0)]) for i in range(tracers) for t in range(tiles)
    }
    at_rim = rim_lanes(lanes)
    placed = {(i, k): edge_at(edge[i, t], s) for t in range(tiles) for s, k in slots[t] for i in range(tracers)}
    for i in range(tracers):
        solved = [
            jnp.where(at_rim, total([weights[n, k] * placed[i, k] for k in range(levels)]), sums[n * tracers + i])
            for n in range(2)
        ]
        first = jnp.where(at_rim, placed[i, 0], lateral[i, 0])
        last = jnp.where(at_rim, placed[i, levels - 1], lateral[i, levels - 1])
        message[i] = rims[0] * solved[1] - rims[2] * last
        message[tracers + 2 + i] = rims[3] * solved[0]
        message[2 * tracers + 2 + i] = rims[3] * first
    message[tracers] = rims[0]
    message[tracers + 1] = rims[1]
    message[3 * tracers + 2] = rims[3]
    message[3 * tracers + 3] = rims[4]
    for i, t in edge:
        edges[i, t] = edge[i, t]


def rim_lanes(lanes):
    return (lanes < SUB) | (lanes >= lanes.shape[1] - SUB)


def edge_at(tile, slot):
    return rolled(tile, -SUB - SLOT * slot, 1)


def total(terms):
    while len(terms) > 1:
        terms = [sum(terms[n : n + 2][1:], terms[n]) for n in range(0, len(terms), 2)]
    return terms[0]


def block_kernel(lateral, edges, down, up, pivots, ratios, couplings, from_first, from_last, kept, base, gain):
    tracers, levels, _, width = lateral.shape
    slots = slots_of(levels, width)
    at_rim = rim_lanes(lanes_of(kept[0]))
    here = {
        (i, k): jnp.where(at_rim, edge_at(edges[i, t], s), lateral[i, k])
        for t in range(len(slots))
        for s, k in slots[t]
        for i in range(tracers)
    }
    values = {}
    for i in range(tracers):
        flux = [down[k] * here[i, k + 1] + up[k] * here[i, k] for k in range(levels - 1)]
        for k in range(levels):
            values[i, k] = here[i, k] if k == levels - 1 else here[i, k] + flux[k]
            if k > 0:
                values[i, k] = values[i, k] - flux[k - 1]
    for i in range(tracers):
        values[i, 0] = values[i, 0] * pivots[0]
    for k in range(1, levels):
        for i in range(tracers):
            values[i, k] = (values[i, k] + couplings[k - 1] * values[i, k - 1]) * pivots[k]
    for k in range(levels - 2, -1, -1):
        for i in range(tracers):
            values[i, k] = values[i, k] + ratios[k] * values[i, k + 1]
    z = lax.axis_index("gz")
    pair = [kept[i] for i in range(tracers)] + [kept[tracers]]
    top = [jnp.where((z == 1) | (z == 3), p, 0.0) for p in pair]
    low = [jnp.where((z == 0) | (z == 2), p, 0.0) for p in pair]
    top_gain = jnp.where(z == 2, 1.0, top[tracers])
    low_gain = jnp.where(z == 1, 1.0, low[tracers])
    for k in range(levels):
        gain[k] = low_gain * from_last[k] - top_gain * from_first[k]
        for i in range(tracers):
            base[i, k] = values[i, k] - top[i] * from_first[k] + low[i] * from_last[k]


def interface(upper, lower, tracers):
    heads, alpha, beta = upper[:tracers], upper[tracers], upper[tracers + 1]
    sums, rims, admit = lower[:tracers], lower[tracers : 2 * tracers], lower[2 * tracers]
    inverse = jnp.where(admit > 0.0, 1.0 / (admit + alpha), 0.0)
    flux = [(alpha * s + beta * r - admit * h) * inverse for s, r, h in zip(sums, rims, heads)]
    return flux, admit * alpha * inverse


def pair_kernel(own, other, merged, kept):
    tracers = kept.shape[0] - 1
    z = lax.axis_index("gz")
    lower_here = z % 2 == 1
    lower_pair = z >= 2
    upper, lower = [], []
    count = own.shape[0]
    for j in range(count):
        upper.append(jnp.where(lower_here, other[j], own[j]))
        lower.append(jnp.where(lower_here, own[j], other[j]))
    n = tracers + 2
    flux, gain = interface(upper[:n], lower[n:-1], tracers)
    across = jnp.where(lower_pair, upper[-1], lower[-1])
    gain = gain * across
    for i in range(tracers):
        kept[i] = flux[i]
    kept[tracers] = gain
    factor = across * jnp.where(lower_pair, upper[-2], lower[tracers])
    scale = 1.0 / (1.0 - factor * gain)
    for i in range(tracers):
        head = jnp.where(lower_pair, upper[n + i] + factor * flux[i], lower[i] - factor * flux[i])
        merged[i] = head * scale
    for i in range(tracers + 1):
        merged[tracers + i] = scale * (
            jnp.where(lower_pair, upper[n + tracers + i], lower[tracers + i] if i < 2 else 0.0)
        )


def final_kernel(own, other, base, gain, out, staged, sems):
    tracers, levels = base.shape[:2]
    lower_pair = lax.axis_index("gz") >= 2
    upper = [jnp.where(lower_pair, other[j], own[j]) for j in range(own.shape[0])]
    lower = [jnp.where(lower_pair, own[j], other[j]) for j in range(own.shape[0])]
    middle, _ = interface(upper[: tracers + 2], lower, tracers)
    copies = []
    for i in range(tracers):
        for k in range(levels):
            staged[i, k] = base[i, k] + middle[i] * gain[k]
        copies.append(pltpu.make_async_copy(staged.at[i], out.at[i], sems.at[i]))
        copies[i].start()
    for copy in copies:
        copy.wait()


def local(
    tracer, east_flow, north_flow, vertical_flow, mixing_lateral, mixing_vertical, sea_mask, bottom
):
    tracers, levels, rows, width = tracer.shape
    arrays = tracers + 4
    tiles = len(slots_of(levels, width))
    assert arrays == 2 * GROUP
    plane = (rows, width)
    block = (levels, rows, width)
    ring = lax.axis_size("gx")
    cells = levels * rows * width
    near_pairs = [(i, i ^ 1) for i in range(ring)]
    far_pairs = [(i, (i + 1) % ring if i % 2 else (i - 1) % ring) for i in range(ring)]

    tracer_here, mixing, east, north, wet, vertical, mixing_down, west_tiles, east_tiles, to_far = call(
        pack_kernel,
        [tracer.shape] + [block] * 6 + [(arrays, tiles) + plane] * 2 + [(2, tiles) + plane],
        20 * cells,
        tracer, mixing_lateral, east_flow, north_flow, sea_mask, bottom, vertical_flow, mixing_vertical,
        in_specs=[HBM] * 8,
        scratch=[
            pltpu.VMEM(block, jnp.int32),
            pltpu.VMEM(plane, jnp.int32),
            pltpu.SemaphoreType.DMA((tracers + 7,)),
        ],
    )
    far = lax.ppermute(to_far, "gx", far_pairs)
    to_near, down, up, from_first, from_last, pivots, ratios, couplings, weights, rims = call(
        side_kernel,
        [(2, tiles) + plane] + [block] * 7 + [(2,) + block, (5,) + plane],
        50 * cells,
        wet, vertical, mixing_down, west_tiles,
    )
    near = lax.ppermute(to_near, "gx", near_pairs)
    lateral, sums = call(
        interior_kernel,
        [tracer.shape, (2 * tracers,) + plane],
        100 * cells,
        tracer_here, mixing, east, north, wet, weights,
    )
    edges, message = call(
        rim_kernel,
        [(tracers, tiles) + plane, (3 * tracers + 4,) + plane],
        20 * cells,
        west_tiles, east_tiles, far, near, lateral, weights, sums, rims,
    )
    other = lax.ppermute(message, "gz", [(i, i ^ 1) for i in range(4)])
    merged, kept = call(
        pair_kernel, [(2 * tracers + 1,) + plane, (tracers + 1,) + plane], cells, message, other
    )
    beyond = lax.ppermute(merged, "gz", [(i, i ^ 2) for i in range(4)])
    base, gain = call(
        block_kernel,
        [tracer.shape, block],
        40 * cells,
        lateral, edges, down, up, pivots, ratios, couplings, from_first, from_last, kept,
    )
    (result,) = call(
        final_kernel, [tracer.shape], 10 * cells, merged, beyond, base, gain,
        out_specs=[HBM],
        scratch=[pltpu.VMEM(tracer.shape, jnp.float32), pltpu.SemaphoreType.DMA((tracers,))],
    )
    return result


def solution(mesh):
    assert mesh.shape["gz"] == 4 and mesh.shape["gx"] % 2 == 0
    return jax.shard_map(
        local,
        mesh=mesh,
        in_specs=(
            P(None, "gz", None, "gx"),
            P("gz", None, "gx"),
            P("gz", None, "gx"),
            P("gz", None, "gx"),
            P("gz", None, "gx"),
            P("gz", None, "gx"),
            P("gz", None, "gx"),
            P(None, "gx"),
        ),
        out_specs=P(None, "gz", None, "gx"),
        check_vma=False,
    )
```

time: 32.5 us -> 18.5 us (0.57)
  Pallas kernels: 13.4 us -> 4.78 us
  local copies, waits for them, and re-layouts: 5.42 us -> 0 us
  starting transfers between devices: 7.7 us -> 9.21 us
  waiting for transfers between devices: 5.63 us -> 4.25 us
    pallas_call x6 -> x7, Pallas kernels: 13.4 us -> 4.78 us  [call(): pl.pallas_call(kernel, out_shape=outs, in_specs=in_specs or [VMEM] * len(...]
    unnamed x16 -> x0, local copies, waits for them, and re-layouts: 5.42 us -> none
    ppermute x1, starting transfers between devices: 1.64 us -> 2.64 us  [local(): other = lax.ppermute(message, 'gz', [(i, i ^ 1) for i in range(4)])]
    ppermute x1, waiting for transfers between devices: 3.27 us -> 2.42 us  [local(): other = lax.ppermute(message, 'gz', [(i, i ^ 1) for i in range(4)])]
    ppermute x1, waiting for transfers between devices: 2.35 us -> 1.62 us  [local(): beyond = lax.ppermute(merged, 'gz', [(i, i ^ 2) for i in range(4)])]
    ppermute x1, starting transfers between devices: 2.65 us -> 3.1 us  [local(): beyond = lax.ppermute(merged, 'gz', [(i, i ^ 2) for i in range(4)])]
  transfers between devices with their start and end apart: 4 -> 4, of which waited for: 2 -> 3; matrix products, arithmetic and copies ran while one was open for 0% -> 0% of each run, Pallas kernels for 35% -> 9%
where the time goes in v2:
time: 18.5 us; the launch traced here: 18.3 us
  starting transfers between devices  9.21 us (50%)
  Pallas kernels  4.78 us (26%)
  waiting for transfers between devices  4.25 us (23%)
    pallas_call x7, Pallas kernels, call(): pl.pallas_call(kernel, out_shape=outs, in_specs=in_specs or [VMEM] * len(...  4.78 us
    ppermute x1, starting transfers between devices, local(): far = lax.ppermute(to_far, 'gx', far_pairs)  3.4 us
    ppermute x1, starting transfers between devices, local(): beyond = lax.ppermute(merged, 'gz', [(i, i ^ 2) for i in range(4)])  3.1 us
    ppermute x1, starting transfers between devices, local(): other = lax.ppermute(message, 'gz', [(i, i ^ 1) for i in range(4)])  2.64 us
    ppermute x1, waiting for transfers between devices, local(): other = lax.ppermute(message, 'gz', [(i, i ^ 1) for i in range(4)])  2.42 us
    ppermute x1, waiting for transfers between devices, local(): beyond = lax.ppermute(merged, 'gz', [(i, i ^ 2) for i in range(4)])  1.62 us
  transfers between devices with their start and end apart: 4, of which 3 were waited for; matrix products, arithmetic and copies ran while one was open for 0% of the time, Pallas kernels for 9%

profile of v2, /device:TPU:0, one launch (start us, length us, event | category | flops | bytes accessed | tf_op | source)
XLA Modules:
  0.0 18.3 jit_solution(8304657873523181659)
XLA Ops:
  0.0 1.8 %shard_map.82 = (f32[2,25,16,128]{3,2,1,0:T(8,128)S(1)}, f32[25,16,128]{2,1,0:T(8,128)S(1)}, f32[25,16,128]{2,1,0:T(8,128)S(1)}, f32[25,16,128]{2,1,0:T(8,128)S(...) custom-call(f32[2,25,16,128]{3,2,1,0:T(8,128)} %tracer_in.1, ...), custom_call_target="tpu_custom_call" | custom-call | flops 1024000 | bytes 3514368 | tf_op jit(solution)/shard_map/pallas_call | solution.py:21
  1.8 3.4 %collective-permute-start = (f32[2,2,16,128]{3,2,1,0:T(8,128)S(1)}, f32[2,2,16,128]{3,2,1,0:T(8,128)S(1)}, u32[]{:S(2)}, u32[]{:S(2)}) collective-permute-start(f32[2,2,16,128]{3,2,1,0:T(8,128)S(1)} %get-tuple-element.35), channel_id=1, source_target_pairs={{0,28},{4,8},{8,4},{12,16},{16,12},{20,24},{24,20},{28,0},{1,29},{... | collective-permute-start | bytes 98312 | tf_op jit(solution)/shard_map/ppermute | solution.py:433
  5.2 0.3 %shard_map.83 = (f32[2,2,16,128]{3,2,1,0:T(8,128)S(1)}, f32[25,16,128]{2,1,0:T(8,128)S(1)}, f32[25,16,128]{2,1,0:T(8,128)S(1)}, f32[25,16,128]{2,1,0:T(8,128)S(1...) custom-call(f32[25,16,128]{2,1,0:T(8,128)S(1)} %get-tuple-element.36, ...), custom_call_target="tpu_custom_call" | custom-call | flops 2560000 | bytes 2629632 | tf_op jit(solution)/shard_map/pallas_call | solution.py:21
  5.5 0.1 collective-permute-start.1
  5.5 1.0 %shard_map.84 = (f32[2,25,16,128]{3,2,1,0:T(8,128)S(1)}, f32[4,16,128]{2,1,0:T(8,128)S(1)}) custom-call(f32[2,25,16,128]{3,2,1,0:T(8,128)S(1)} %get-tuple-element.40.tracer, f32[25,16,128]{2,1,0:T(8,128)S(1)} %get-tuple-element.41.mixing, f32[25,16,128]{2,1,0:T(8,128)S(1)} %get-tuple-element.42.east, f32[25,16,128]{2,1,0:T(8,128)S(1)} %get-tuple-element.43.north, ...), custom_call_target="tpu_custom_call" | custom-call | flops 5120000 | bytes 2080768 | tf_op jit(solution)/shard_map/pallas_call | solution.py:21
  6.6 0.2 %collective-permute-done.far = f32[2,2,16,128]{3,2,1,0:T(8,128)S(1)} collective-permute-done((f32[2,2,16,128]{3,2,1,0:T(8,128)S(1)}, f32[2,2,16,128]{3,2,1,0:T(8,128)S(1)}, u32[]{:S(2)}, u32[]{:S(2)}) %collective-permute-start) | collective-permute-done | bytes 32800 | tf_op jit(solution)/shard_map/ppermute | solution.py:433
  6.8 0.0 collective-permute-done.1.near
  6.8 0.5 %shard_map.85 = (f32[2,2,16,128]{3,2,1,0:T(8,128)S(1)}, f32[10,16,128]{2,1,0:T(8,128)S(1)}) custom-call(f32[6,2,16,128]{3,2,1,0:T(8,128)S(1)} %get-tuple-element.33.west_tiles, f32[6,2,16,128]{3,2,1,0:T(8,128)S(1)} %get-tuple-element.34.east_tiles, f32[2,2,16,128]{3,2,1,0:T(8,128)S(1)} %collective-permute-done.far, ...), custom_call_target="tpu_custom_call" | custom-call | flops 1024000 | bytes 1269760 | tf_op jit(solution)/shard_map/pallas_call | solution.py:21
  7.3 2.6 %collective-permute-start.2 = (f32[10,16,128]{2,1,0:T(8,128)S(1)}, f32[10,16,128]{2,1,0:T(8,128)S(1)}, u32[]{:S(2)}, u32[]{:S(2)}) collective-permute-start(f32[10,16,128]{2,1,0:T(8,128)S(1)} %get-tuple-element.48.own), channel_id=1, source_target_pairs={{0,1},{1,0},{2,3},{3,2},{4,5},{5,4},{6,7},{7,6},{8,9},{9,8},{10,11... | collective-permute-start | bytes 245768 | tf_op jit(solution)/shard_map/ppermute | solution.py:453
  9.9 2.4 %collective-permute-done.2.other = f32[10,16,128]{2,1,0:T(8,128)S(1)} collective-permute-done((f32[10,16,128]{2,1,0:T(8,128)S(1)}, f32[10,16,128]{2,1,0:T(8,128)S(1)}, u32[]{:S(2)}, u32[]{:S(2)}) %collective-permute-start.2) | collective-permute-done | bytes 81952 | tf_op jit(solution)/shard_map/ppermute | solution.py:453
  12.4 3.1 %collective-permute-start.3 = (f32[5,16,128]{2,1,0:T(8,128)S(1)}, f32[5,16,128]{2,1,0:T(8,128)S(1)}, u32[]{:S(2)}, u32[]{:S(2)}) collective-permute-start(f32[5,16,128]{2,1,0:T(8,128)S(1)} %get-tuple-element.49.own), channel_id=1, source_target_pairs={{0,2},{1,3},{2,0},{3,1},{4,6},{5,7},{6,4},{7,5},{8,10},{9,11},{10,... | collective-permute-start | bytes 122888 | tf_op jit(solution)/shard_map/ppermute | solution.py:457
  15.5 0.4 %shard_map.87 = (f32[2,25,16,128]{3,2,1,0:T(8,128)S(1)}, f32[25,16,128]{2,1,0:T(8,128)S(1)}) custom-call(f32[2,25,16,128]{3,2,1,0:T(8,128)S(1)} %get-tuple-element.45.lateral, f32[2,2,16,128]{3,2,1,0:T(8,128)S(1)} %get-tuple-element.50.edges, f32[25,16,128]{2,1,0:T(8,128)S(1)} %get-tuple-element.51.down, f32[25,16,128]{2,1,0:T(8,128)S(1)} %get-tuple-element.52.up, ...), custom_call_target="tpu_custom_call" | custom-call | flops 2048000 | bytes 2514944 | tf_op jit(solution)/shard_map/pallas_call | solution.py:21
  15.9 1.6 %collective-permute-done.3.other = f32[5,16,128]{2,1,0:T(8,128)S(1)} collective-permute-done((f32[5,16,128]{2,1,0:T(8,128)S(1)}, f32[5,16,128]{2,1,0:T(8,128)S(1)}, u32[]{:S(2)}, u32[]{:S(2)}) %collective-permute-start.3) | collective-permute-done | bytes 40992 | tf_op jit(solution)/shard_map/ppermute | solution.py:457
  17.5 0.8 %shard_map.88 = f32[2,25,16,128]{3,2,1,0:T(8,128)} custom-call(f32[5,16,128]{2,1,0:T(8,128)S(1)} %get-tuple-element.49.own, f32[5,16,128]{2,1,0:T(8,128)S(1)} %collective-permute-done.3.other, f32[2,25,16,128]{3,2,1,0:T(8,128)S(1)} %get-tuple-element.59.base, f32[25,16,128]{2,1,0:T(8,128)S(1)} %get-tuple-element.60.gain), custom_call_target="tpu_custom_call" | custom-call | flops 512000 | bytes 1105920 | tf_op jit(solution)/shard_map/pallas_call | solution.py:21
  (1 shorter events, 0.0 us)
Async XLA Ops:
  1.8 5.0 %collective-permute-start = (f32[2,2,16,128]{3,2,1,0:T(8,128)S(1)}, f32[2,2,16,128]{3,2,1,0:T(8,128)S(1)}, u32[]{:S(2)}, u32[]{:S(2)}) collective-permute-start(f32[2,2,16,128]{3,2,1,0:T(8,128)S(1)} %get-tuple-element.35), channel_id=1, source_target_pairs={{0,28},{4,8},{8,4},{12,16},{16,12},{20,24},{24,20},{28,0},{1,29},{... | collective-permute-start | bytes 98312 | tf_op jit(solution)/shard_map/ppermute | solution.py:433
  5.5 1.3 %collective-permute-start.1 = (f32[2,2,16,128]{3,2,1,0:T(8,128)S(1)}, f32[2,2,16,128]{3,2,1,0:T(8,128)S(1)}, u32[]{:S(2)}, u32[]{:S(2)}) collective-permute-start(f32[2,2,16,128]{3,2,1,0:T(8,128)S(1)} %get-tuple-element.39), channel_id=1, source_target_pairs={{0,4},{4,0},{8,12},{12,8},{16,20},{20,16},{24,28},{28,24},{1,5},{5... | collective-permute-start | bytes 98312 | tf_op jit(solution)/shard_map/ppermute | solution.py:440
  7.3 5.1 %collective-permute-start.2 = (f32[10,16,128]{2,1,0:T(8,128)S(1)}, f32[10,16,128]{2,1,0:T(8,128)S(1)}, u32[]{:S(2)}, u32[]{:S(2)}) collective-permute-start(f32[10,16,128]{2,1,0:T(8,128)S(1)} %get-tuple-element.48.own), channel_id=1, source_target_pairs={{0,1},{1,0},{2,3},{3,2},{4,5},{5,4},{6,7},{7,6},{8,9},{9,8},{10,11... | collective-permute-start | bytes 245768 | tf_op jit(solution)/shard_map/ppermute | solution.py:453
  12.4 5.1 %collective-permute-start.3 = (f32[5,16,128]{2,1,0:T(8,128)S(1)}, f32[5,16,128]{2,1,0:T(8,128)S(1)}, u32[]{:S(2)}, u32[]{:S(2)}) collective-permute-start(f32[5,16,128]{2,1,0:T(8,128)S(1)} %get-tuple-element.49.own), channel_id=1, source_target_pairs={{0,2},{1,3},{2,0},{3,1},{4,6},{5,7},{6,4},{7,5},{8,10},{9,11},{10,... | collective-permute-start | bytes 122888 | tf_op jit(solution)/shard_map/ppermute | solution.py:457

commit v3 on v2

--- a/solution.py
+++ b/solution.py
@@ -30,11 +30,19 @@
 
 
 def rolled(plane, shift, axis):
-    return pltpu.roll(plane, shift % plane.shape[axis], axis)
+    shift = shift % plane.shape[axis]
+    return pltpu.roll(plane, shift, axis) if shift else plane
 
 
 def lanes_of(plane):
     return lax.broadcasted_iota(jnp.int32, plane.shape, 1)
+
+
+def places_of(plane, behind):
+    factor = -(-512 // SLOT)
+    assert all(n * factor >> 9 == n // SLOT for n in range(plane.shape[1] + SLOT))
+    lane = lanes_of(plane) + jnp.where(behind, SLOT - SUB, 0)
+    return lane - SLOT * ((lane * factor) >> 9)
 
 
 def lateral_coefficients(east, north, mixing, wet):
@@ -123,29 +131,50 @@
 
 
 def pack_group(tiles, first_columns):
-    lane = lax.rem(lanes_of(tiles[0]), SLOT)
-    packed = None
-    for q, tile in enumerate(tiles):
-        moved = jnp.where(first_columns, rolled(tile, SUB * (q - 1), 1), rolled(tile, SUB * q, 1))
-        packed = moved if q == 0 else jnp.where(lane >= SUB * q, moved, packed)
+    place = places_of(tiles[0], first_columns)
+    packed = tiles[0]
+    for q, tile in enumerate(tiles[1:], 1):
+        packed = jnp.where(place >= SUB * q, rolled(tile, SUB * q, 1), packed)
     return packed
+
+
+def window_results(own, received, behind, tracers):
+    theirs = places_of(own[0, 0], behind) < SUB
+    windows = {}
+    for j, t in own:
+        g, q = divmod(j, GROUP)
+        windows[j, t] = jnp.where(theirs, rolled(received[g, t], -SUB * q, 1), own[j, t])
+    stencils = {t: stencil(*(windows[tracers + j, t] for j in (2, 3, 0, 1))) for j, t in own if j == 0}
+    return stencil_substeps({(j, t): windows[j, t] for j, t in own if j < tracers}, stencils)
 
 
 def pack_kernel(
     tracer_in, mixing_in, east_in, north_in, mask_in, bottom_in, vertical_in, mixing_vertical_in,
-    tracer, mixing, east, north, wet, vertical, mixing_vertical, west_tiles, east_tiles, to_far, mask, bottom, sems,
+    tracer, mixing, east, north, wet, vertical, mixing_vertical, west_tiles, east_tiles, to_far, to_near, mask, bottom, sems,
 ):
     levels, _, width = mask.shape
     tracers = tracer.shape[0]
-    pairs = [(bottom_in, bottom), (mask_in, mask), (mixing_in, mixing), (east_in, east), (north_in, north)]
-    pairs += [(tracer_in.at[i], tracer.at[i]) for i in range(tracers)]
+    pairs = [(tracer_in.at[i], tracer.at[i]) for i in range(tracers)]
+    pairs += [(east_in, east), (bottom_in, bottom), (mask_in, mask), (north_in, north), (mixing_in, mixing)]
     pairs += [(vertical_in, vertical), (mixing_vertical_in, mixing_vertical)]
     copies = [pltpu.make_async_copy(source, target, sems.at[n]) for n, (source, target) in enumerate(pairs)]
     for copy in copies:
         copy.start()
     slots = slots_of(levels, width)
     even = lax.axis_index("gx") % 2 == 0
-    for copy in copies[:4]:
+    found = {}
+
+    def find(j, t, pair):
+        found[j, t] = pair[0]
+        west_tiles[j, t], east_tiles[j, t] = pair
+
+    for copy in copies[: tracers + 1]:
+        copy.wait()
+    for t, part in enumerate(slots):
+        for i in range(tracers):
+            find(i, t, window_tiles(lambda k: tracer[i, k], part))
+        find(tracers + 2, t, window_tiles(lambda k: east[k], part))
+    for copy in copies[tracers + 1 : -2]:
         copy.wait()
     floor = bottom[...] - lax.axis_index("gz") * levels
     signed = []
@@ -153,50 +182,49 @@
         is_wet = (mask[k] > 0) & (k < floor)
         wet[k] = jnp.where(is_wet, 1.0, 0.0)
         signed.append(jnp.where(is_wet, mixing[k], -mixing[k]))
-    found = {}
-
-    def find(j, t, pair):
-        found[j, t] = pair[0]
-        west_tiles[j, t], east_tiles[j, t] = pair
-
     for t, part in enumerate(slots):
         both = window_tiles(lambda k: signed[k], part)
         find(tracers, t, [jnp.abs(b) for b in both])
         find(tracers + 1, t, [jnp.where(b > 0.0, 1.0, 0.0) for b in both])
-        find(tracers + 2, t, window_tiles(lambda k: east[k], part))
-    for copy in copies[4:-2]:
-        copy.wait()
-    for t, part in enumerate(slots):
-        for i in range(tracers):
-            find(i, t, window_tiles(lambda k: tracer[i, k], part))
         find(tracers + 3, t, window_tiles(lambda k: north[k], part))
     for t in range(len(slots)):
         for g in range(to_far.shape[0]):
-            to_far[g, t] = pack_group([found[g * GROUP + q, t] for q in range(GROUP)], even)
+            group = [found[g * GROUP + q, t] for q in range(GROUP)]
+            to_far[g, t] = pack_group(group, even)
+            to_near[g, t] = pack_group(group, jnp.logical_not(even))
     for copy in copies[-2:]:
         copy.wait()
 
 
 def side_kernel(
-    wet, vertical, mixing_vertical, west_tiles,
-    to_near, down, up, from_first, from_last, pivots, ratios, couplings, weights, rims,
+    wet, vertical, mixing_vertical,
+    down, up, from_first, from_last, pivots, ratios, couplings, weights, rims,
 ):
-    odd = lax.axis_index("gx") % 2 == 1
-    for g, t in [(g, t) for g in range(to_near.shape[0]) for t in range(to_near.shape[1])]:
-        to_near[g, t] = pack_group([west_tiles[g * GROUP + q, t] for q in range(GROUP)], odd)
     vertical_statics(
         wet, vertical, mixing_vertical, down, up, from_first, from_last, pivots, ratios, couplings, weights, rims
     )
 
 
-def interior_kernel(tracer, mixing, east, north, wet, weights, lateral, sums):
+def interior_kernel(
+    tracer, mixing, east, north, wet, weights, west_tiles, east_tiles, near, lateral, sums, near_edges, far_tiles
+):
     levels = wet.shape[0]
     tracers = tracer.shape[0]
+    arrays, tiles = east_tiles.shape[:2]
+    even = lax.axis_index("gx") % 2 == 0
+    own, received = {}, {(g, t): near[g, t] for g in range(near.shape[0]) for t in range(tiles)}
+    for j in range(arrays):
+        for t in range(tiles):
+            own[j, t] = jnp.where(even, east_tiles[j, t], west_tiles[j, t])
+            far_tiles[j, t] = jnp.where(even, west_tiles[j, t], east_tiles[j, t])
+    done = window_results(own, received, even, tracers)
     coefficients = {k: lateral_coefficients(east[k], north[k], mixing[k], wet[k]) for k in range(levels)}
     planes = {(i, k): tracer[i, k] for k in range(levels) for i in range(tracers)}
     planes = lateral_substeps(planes, coefficients)
     for i, k in planes:
         lateral[i, k] = planes[i, k]
+    for i, t in done:
+        near_edges[i, t] = done[i, t]
     for i in range(tracers):
         for n in range(2):
             sums[n * tracers + i] = total([weights[n, k] * planes[i, k] for k in range(levels)])
@@ -258,29 +286,17 @@
         rims[n] = value
 
 
-def rim_kernel(west_tiles, east_tiles, far, near, lateral, weights, sums, rims, edges, message):
+def rim_kernel(far_tiles, far, near_edges, lateral, weights, sums, rims, edges, message):
     tracers, levels, _, width = lateral.shape
-    even = lax.axis_index("gx") % 2 == 0
+    odd = lax.axis_index("gx") % 2 == 1
     slots = slots_of(levels, width)
-    arrays, tiles = east_tiles.shape[:2]
+    arrays, tiles = far_tiles.shape[:2]
     lanes = lanes_of(rims[0])
-    lane = lax.rem(lanes, SLOT)
-    windows = {}
-    for t in range(tiles):
-        from_west = [jnp.where(even, far[g, t], near[g, t]) for g in range(far.shape[0])]
-        from_east = [jnp.where(even, near[g, t], far[g, t]) for g in range(far.shape[0])]
-        for j in range(arrays):
-            g, q = divmod(j, GROUP)
-            windows[j, t, 0] = jnp.where(lane < SUB, rolled(from_west[g], -SUB * q, 1), west_tiles[j, t])
-            windows[j, t, 1] = jnp.where(
-                (lane >= SUB) & (lane < 2 * SUB), rolled(from_east[g], SUB * (1 - q), 1), east_tiles[j, t]
-            )
-    places = [(t, side) for t in range(tiles) for side in range(2)]
-    stencils = {p: stencil(*(windows[(tracers + j,) + p] for j in (2, 3, 0, 1))) for p in places}
-    done = stencil_substeps({(i, p): windows[(i,) + p] for p in places for i in range(tracers)}, stencils)
-    edge = {
-        (i, t): jnp.where(lane < SUB, done[i, (t, 1)], done[i, (t, 0)]) for i in range(tracers) for t in range(tiles)
-    }
+    own = {(j, t): far_tiles[j, t] for j in range(arrays) for t in range(tiles)}
+    received = {(g, t): far[g, t] for g in range(far.shape[0]) for t in range(tiles)}
+    done = window_results(own, received, odd, tracers)
+    from_far = places_of(rims[0], jnp.logical_not(odd)) < SUB
+    edge = {(i, t): jnp.where(from_far, done[i, t], near_edges[i, t]) for i, t in done}
     at_rim = rim_lanes(lanes)
     placed = {(i, k): edge_at(edge[i, t], s) for t in range(tiles) for s, k in slots[t] for i in range(tracers)}
     for i in range(tracers):
@@ -418,9 +434,9 @@
     near_pairs = [(i, i ^ 1) for i in range(ring)]
     far_pairs = [(i, (i + 1) % ring if i % 2 else (i - 1) % ring) for i in range(ring)]
 
-    tracer_here, mixing, east, north, wet, vertical, mixing_down, west_tiles, east_tiles, to_far = call(
+    tracer_here, mixing, east, north, wet, vertical, mixing_down, west_tiles, east_tiles, to_far, to_near = call(
         pack_kernel,
-        [tracer.shape] + [block] * 6 + [(arrays, tiles) + plane] * 2 + [(2, tiles) + plane],
+        [tracer.shape] + [block] * 6 + [(arrays, tiles) + plane] * 2 + [(2, tiles) + plane] * 2,
         20 * cells,
         tracer, mixing_lateral, east_flow, north_flow, sea_mask, bottom, vertical_flow, mixing_vertical,
         in_specs=[HBM] * 8,
@@ -431,24 +447,24 @@
         ],
     )
     far = lax.ppermute(to_far, "gx", far_pairs)
-    to_near, down, up, from_first, from_last, pivots, ratios, couplings, weights, rims = call(
+    near = lax.ppermute(to_near, "gx", near_pairs)
+    down, up, from_first, from_last, pivots, ratios, couplings, weights, rims = call(
         side_kernel,
-        [(2, tiles) + plane] + [block] * 7 + [(2,) + block, (5,) + plane],
+        [block] * 7 + [(2,) + block, (5,) + plane],
         50 * cells,
-        wet, vertical, mixing_down, west_tiles,
-    )
-    near = lax.ppermute(to_near, "gx", near_pairs)
-    lateral, sums = call(
+        wet, vertical, mixing_down,
+    )
+    lateral, sums, near_edges, far_tiles = call(
         interior_kernel,
-        [tracer.shape, (2 * tracers,) + plane],
+        [tracer.shape, (2 * tracers,) + plane, (tracers, tiles) + plane, (arrays, tiles) + plane],
         100 * cells,
-        tracer_here, mixing, east, north, wet, weights,
+        tracer_here, mixing, east, north, wet, weights, west_tiles, east_tiles, near,
     )
     edges, message = call(
         rim_kernel,
         [(tracers, tiles) + plane, (3 * tracers + 4,) + plane],
         20 * cells,
-        west_tiles, east_tiles, far, near, lateral, weights, sums, rims,
+        far_tiles, far, near_edges, lateral, weights, sums, rims,
     )
     other = lax.ppermute(message, "gz", [(i, i ^ 1) for i in range(4)])
     merged, kept = call(

time: 18.5 us -> 18.3 us (0.989)
  starting transfers between devices: 9.21 us -> 8.69 us
  waiting for transfers between devices: 4.25 us -> 4.64 us
    ppermute x1, starting transfers between devices: 2.64 us -> 1.8 us  [local(): other = lax.ppermute(message, 'gz', [(i, i ^ 1) for i in range(4)])]
    ppermute x1, starting transfers between devices: 0.07 us -> 0.52 us  [local(): near = lax.ppermute(to_near, 'gx', near_pairs)]
    ppermute x1, starting transfers between devices: 3.1 us -> 2.81 us  [local(): beyond = lax.ppermute(merged, 'gz', [(i, i ^ 2) for i in range(4)])]
    ppermute x1, waiting for transfers between devices: 2.42 us -> 2.71 us  [local(): other = lax.ppermute(message, 'gz', [(i, i ^ 1) for i in range(4)])]
  transfers between devices with their start and end apart: 4 -> 4, of which waited for: 3 -> 3; matrix products, arithmetic and copies ran while one was open for 0% -> 0% of each run, Pallas kernels for 9% -> 10%
where the time goes in v3:
time: 18.3 us; the launch traced here: 18.2 us
  starting transfers between devices  8.69 us (47%)
  Pallas kernels  4.83 us (26%)
  waiting for transfers between devices  4.64 us (25%)
    pallas_call x7, Pallas kernels, call(): pl.pallas_call(kernel, out_shape=outs, in_specs=in_specs or [VMEM] * len(...  4.83 us
    ppermute x1, starting transfers between devices, local(): far = lax.ppermute(to_far, 'gx', far_pairs)  3.56 us
    ppermute x1, starting transfers between devices, local(): beyond = lax.ppermute(merged, 'gz', [(i, i ^ 2) for i in range(4)])  2.81 us
    ppermute x1, waiting for transfers between devices, local(): other = lax.ppermute(message, 'gz', [(i, i ^ 1) for i in range(4)])  2.71 us
    ppermute x1, starting transfers between devices, local(): other = lax.ppermute(message, 'gz', [(i, i ^ 1) for i in range(4)])  1.8 us
    ppermute x1, waiting for transfers between devices, local(): beyond = lax.ppermute(merged, 'gz', [(i, i ^ 2) for i in range(4)])  1.79 us
    ppermute x1, starting transfers between devices, local(): near = lax.ppermute(to_near, 'gx', near_pairs)  0.52 us
  transfers between devices with their start and end apart: 4, of which 3 were waited for; matrix products, arithmetic and copies ran while one was open for 0% of the time, Pallas kernels for 10%

profile of v3, /device:TPU:0, one launch (start us, length us, event | category | flops | bytes accessed | tf_op | source)
XLA Modules:
  0.0 18.2 jit_solution(4789662879792905569)
XLA Ops:
  0.0 1.7 %shard_map.82 = (f32[2,25,16,128]{3,2,1,0:T(8,128)S(1)}, f32[25,16,128]{2,1,0:T(8,128)S(1)}, f32[25,16,128]{2,1,0:T(8,128)S(1)}, f32[25,16,128]{2,1,0:T(8,128)S(...) custom-call(f32[2,25,16,128]{3,2,1,0:T(8,128)} %tracer_in.1, ...), custom_call_target="tpu_custom_call" | custom-call | flops 1024000 | bytes 3547136 | tf_op jit(solution)/shard_map/pallas_call | solution.py:21
  1.7 0.5 %collective-permute-start = (f32[2,2,16,128]{3,2,1,0:T(8,128)S(1)}, f32[2,2,16,128]{3,2,1,0:T(8,128)S(1)}, u32[]{:S(2)}, u32[]{:S(2)}) collective-permute-start(f32[2,2,16,128]{3,2,1,0:T(8,128)S(1)} %get-tuple-element.45), channel_id=1, source_target_pairs={{0,4},{4,0},{8,12},{12,8},{16,20},{20,16},{24,28},{28,24},{1,5},{5... | collective-permute-start | bytes 98312 | tf_op jit(solution)/shard_map/ppermute | solution.py:450
  2.2 3.6 %collective-permute-start.1 = (f32[2,2,16,128]{3,2,1,0:T(8,128)S(1)}, f32[2,2,16,128]{3,2,1,0:T(8,128)S(1)}, u32[]{:S(2)}, u32[]{:S(2)}) collective-permute-start(f32[2,2,16,128]{3,2,1,0:T(8,128)S(1)} %get-tuple-element.47), channel_id=1, source_target_pairs={{0,28},{4,8},{8,4},{12,16},{16,12},{20,24},{24,20},{28,0},{1,29},{... | collective-permute-start | bytes 98312 | tf_op jit(solution)/shard_map/ppermute | solution.py:449
  5.8 0.3 %shard_map.83 = (f32[25,16,128]{2,1,0:T(8,128)S(1)}, f32[25,16,128]{2,1,0:T(8,128)S(1)}, f32[25,16,128]{2,1,0:T(8,128)S(1)}, f32[25,16,128]{2,1,0:T(8,128)S(1)},...) custom-call(f32[25,16,128]{2,1,0:T(8,128)S(1)} %get-tuple-element.39, ...), custom_call_target="tpu_custom_call" | custom-call | flops 2560000 | bytes 2498560 | tf_op jit(solution)/shard_map/pallas_call | solution.py:21
  6.1 0.0 collective-permute-done.near
  6.1 1.2 %shard_map.84 = (f32[2,25,16,128]{3,2,1,0:T(8,128)S(1)}, f32[4,16,128]{2,1,0:T(8,128)S(1)}, f32[2,2,16,128]{3,2,1,0:T(8,128)S(1)}, f32[6,2,16,128]{3,2,1,0:T(8,128)S(1)}) custom-call(f32[2,25,16,128]{3,2,1,0:T(8,128)S(1)} %get-tuple-element.35.tracer, f32[25,16,128]{2,1,0:T(8,128)S(1)} %get-tuple-element.36.mixing, ...), custom_call_target="tpu_custom_call" | custom-call | flops 5120000 | bytes 2441216 | tf_op jit(solution)/shard_map/pallas_call | solution.py:21
  7.2 0.1 collective-permute-done.1.far
  7.4 0.5 %shard_map.85 = (f32[2,2,16,128]{3,2,1,0:T(8,128)S(1)}, f32[10,16,128]{2,1,0:T(8,128)S(1)}) custom-call(f32[6,2,16,128]{3,2,1,0:T(8,128)S(1)} %get-tuple-element.46.far_tiles, f32[2,2,16,128]{3,2,1,0:T(8,128)S(1)} %collective-permute-done.1.far, f32[2,2,16,128]{3,2,1,0:T(8,128)S(1)} %get-tuple-element.48.near_edges, ...), custom_call_target="tpu_custom_call" | custom-call | flops 1024000 | bytes 1171456 | tf_op jit(solution)/shard_map/pallas_call | solution.py:21
  7.9 1.8 %collective-permute-start.2 = (f32[10,16,128]{2,1,0:T(8,128)S(1)}, f32[10,16,128]{2,1,0:T(8,128)S(1)}, u32[]{:S(2)}, u32[]{:S(2)}) collective-permute-start(f32[10,16,128]{2,1,0:T(8,128)S(1)} %get-tuple-element.52.own), channel_id=1, source_target_pairs={{0,1},{1,0},{2,3},{3,2},{4,5},{5,4},{6,7},{7,6},{8,9},{9,8},{10,11... | collective-permute-start | bytes 245768 | tf_op jit(solution)/shard_map/ppermute | solution.py:469
  9.7 2.7 %collective-permute-done.2.other = f32[10,16,128]{2,1,0:T(8,128)S(1)} collective-permute-done((f32[10,16,128]{2,1,0:T(8,128)S(1)}, f32[10,16,128]{2,1,0:T(8,128)S(1)}, u32[]{:S(2)}, u32[]{:S(2)}) %collective-permute-start.2) | collective-permute-done | bytes 81952 | tf_op jit(solution)/shard_map/ppermute | solution.py:469
  12.4 2.8 %collective-permute-start.3 = (f32[5,16,128]{2,1,0:T(8,128)S(1)}, f32[5,16,128]{2,1,0:T(8,128)S(1)}, u32[]{:S(2)}, u32[]{:S(2)}) collective-permute-start(f32[5,16,128]{2,1,0:T(8,128)S(1)} %get-tuple-element.53.own), channel_id=1, source_target_pairs={{0,2},{1,3},{2,0},{3,1},{4,6},{5,7},{6,4},{7,5},{8,10},{9,11},{10,... | collective-permute-start | bytes 122888 | tf_op jit(solution)/shard_map/ppermute | solution.py:473
  15.2 0.4 %shard_map.87 = (f32[2,25,16,128]{3,2,1,0:T(8,128)S(1)}, f32[25,16,128]{2,1,0:T(8,128)S(1)}) custom-call(f32[2,25,16,128]{3,2,1,0:T(8,128)S(1)} %get-tuple-element.49.lateral, f32[2,2,16,128]{3,2,1,0:T(8,128)S(1)} %get-tuple-element.54.edges, f32[25,16,128]{2,1,0:T(8,128)S(1)} %get-tuple-element.55.down, f32[25,16,128]{2,1,0:T(8,128)S(1)} %get-tuple-element.56.up, ...), custom_call_target="tpu_custom_call" | custom-call | flops 2048000 | bytes 2514944 | tf_op jit(solution)/shard_map/pallas_call | solution.py:21
  15.6 1.8 %collective-permute-done.3.other = f32[5,16,128]{2,1,0:T(8,128)S(1)} collective-permute-done((f32[5,16,128]{2,1,0:T(8,128)S(1)}, f32[5,16,128]{2,1,0:T(8,128)S(1)}, u32[]{:S(2)}, u32[]{:S(2)}) %collective-permute-start.3) | collective-permute-done | bytes 40992 | tf_op jit(solution)/shard_map/ppermute | solution.py:473
  17.4 0.8 %shard_map.88 = f32[2,25,16,128]{3,2,1,0:T(8,128)} custom-call(f32[5,16,128]{2,1,0:T(8,128)S(1)} %get-tuple-element.53.own, f32[5,16,128]{2,1,0:T(8,128)S(1)} %collective-permute-done.3.other, f32[2,25,16,128]{3,2,1,0:T(8,128)S(1)} %get-tuple-element.63.base, f32[25,16,128]{2,1,0:T(8,128)S(1)} %get-tuple-element.64.gain), custom_call_target="tpu_custom_call" | custom-call | flops 512000 | bytes 1105920 | tf_op jit(solution)/shard_map/pallas_call | solution.py:21
  (1 shorter events, 0.0 us)
Async XLA Ops:
  1.7 4.3 %collective-permute-start = (f32[2,2,16,128]{3,2,1,0:T(8,128)S(1)}, f32[2,2,16,128]{3,2,1,0:T(8,128)S(1)}, u32[]{:S(2)}, u32[]{:S(2)}) collective-permute-start(f32[2,2,16,128]{3,2,1,0:T(8,128)S(1)} %get-tuple-element.45), channel_id=1, source_target_pairs={{0,4},{4,0},{8,12},{12,8},{16,20},{20,16},{24,28},{28,24},{1,5},{5... | collective-permute-start | bytes 98312 | tf_op jit(solution)/shard_map/ppermute | solution.py:450
  2.2 5.2 %collective-permute-start.1 = (f32[2,2,16,128]{3,2,1,0:T(8,128)S(1)}, f32[2,2,16,128]{3,2,1,0:T(8,128)S(1)}, u32[]{:S(2)}, u32[]{:S(2)}) collective-permute-start(f32[2,2,16,128]{3,2,1,0:T(8,128)S(1)} %get-tuple-element.47), channel_id=1, source_target_pairs={{0,28},{4,8},{8,4},{12,16},{16,12},{20,24},{24,20},{28,0},{1,29},{... | collective-permute-start | bytes 98312 | tf_op jit(solution)/shard_map/ppermute | solution.py:449
  7.9 4.5 %collective-permute-start.2 = (f32[10,16,128]{2,1,0:T(8,128)S(1)}, f32[10,16,128]{2,1,0:T(8,128)S(1)}, u32[]{:S(2)}, u32[]{:S(2)}) collective-permute-start(f32[10,16,128]{2,1,0:T(8,128)S(1)} %get-tuple-element.52.own), channel_id=1, source_target_pairs={{0,1},{1,0},{2,3},{3,2},{4,5},{5,4},{6,7},{7,6},{8,9},{9,8},{10,11... | collective-permute-start | bytes 245768 | tf_op jit(solution)/shard_map/ppermute | solution.py:469
  12.4 5.0 %collective-permute-start.3 = (f32[5,16,128]{2,1,0:T(8,128)S(1)}, f32[5,16,128]{2,1,0:T(8,128)S(1)}, u32[]{:S(2)}, u32[]{:S(2)}) collective-permute-start(f32[5,16,128]{2,1,0:T(8,128)S(1)} %get-tuple-element.53.own), channel_id=1, source_target_pairs={{0,2},{1,3},{2,0},{3,1},{4,6},{5,7},{6,4},{7,5},{8,10},{9,11},{10,... | collective-permute-start | bytes 122888 | tf_op jit(solution)/shard_map/ppermute | solution.py:473

commit v4 on v3

--- a/solution.py
+++ b/solution.py
@@ -38,10 +38,10 @@
     return lax.broadcasted_iota(jnp.int32, plane.shape, 1)
 
 
-def places_of(plane, behind):
+def places_of(plane, behind, ahead=0):
     factor = -(-512 // SLOT)
-    assert all(n * factor >> 9 == n // SLOT for n in range(plane.shape[1] + SLOT))
-    lane = lanes_of(plane) + jnp.where(behind, SLOT - SUB, 0)
+    assert all(n * factor >> 9 == n // SLOT for n in range(plane.shape[1] + 2 * SLOT))
+    lane = lanes_of(plane) + jnp.where(behind, SLOT - SUB, 0) + (SLOT + ahead) % SLOT
     return lane - SLOT * ((lane * factor) >> 9)
 
 
@@ -75,11 +75,11 @@
     return planes
 
 
-def stencil(east, north, mixing, wet):
+def stencil(east, north, mixing, wet, beside):
     rows = east.shape[0]
-    wet_west, mixing_west, east_west = (rolled(x, 1, 1) for x in (wet, mixing, east))
-    open_east = wet * rolled(wet, -1, 1)
-    mean_east = 0.5 * (mixing + rolled(mixing, -1, 1))
+    wet_east, wet_west, mixing_east, mixing_west, east_west = beside
+    open_east = wet * wet_east
+    mean_east = 0.5 * (mixing + mixing_east)
     open_west = wet * wet_west
     mean_west = 0.5 * (mixing + mixing_west)
     row = lax.broadcasted_iota(jnp.int32, wet.shape, 0)
@@ -97,12 +97,17 @@
     return here, east_in, west_in, north_in, south_in
 
 
-def stencil_substeps(planes, weights):
-    for _ in range(SUB):
-        sides = {q: (rolled(c, -1, 1), rolled(c, 1, 1), rolled(c, -1, 0), rolled(c, 1, 0)) for q, c in planes.items()}
+def stencil_substeps(planes, weights, beside):
+    for step in range(SUB):
+        if step > 0:
+            beside = {(q, d): rolled(c, d, 1) for q, c in planes.items() for d in (-1, 1)}
         planes = {
-            q: (weights[q[1]][0] * c + weights[q[1]][3] * sides[q][2] + weights[q[1]][4] * sides[q][3])
-            + (weights[q[1]][1] * sides[q][0] + weights[q[1]][2] * sides[q][1])
+            q: (
+                weights[q[1]][0] * c
+                + weights[q[1]][3] * rolled(c, -1, 0)
+                + weights[q[1]][4] * rolled(c, 1, 0)
+            )
+            + (weights[q[1]][1] * beside[q, -1] + weights[q[1]][2] * beside[q, 1])
             for q, c in planes.items()
         }
     return planes
@@ -138,14 +143,33 @@
     return packed
 
 
-def window_results(own, received, behind, tracers):
-    theirs = places_of(own[0, 0], behind) < SUB
-    windows = {}
-    for j, t in own:
+def moved_pairs(tracers):
+    mixing, wet, east = tracers, tracers + 1, tracers + 2
+    return [(i, d) for i in range(tracers) for d in (-1, 1)] + [(wet, -1), (wet, 1), (mixing, -1), (mixing, 1), (east, 1)]
+
+
+def window_results(own, received, behind, tracers, own_moved=None):
+    tiles = [t for j, t in own if j == 0]
+
+    def joined(j, t, d, mine):
         g, q = divmod(j, GROUP)
-        windows[j, t] = jnp.where(theirs, rolled(received[g, t], -SUB * q, 1), own[j, t])
-    stencils = {t: stencil(*(windows[tracers + j, t] for j in (2, 3, 0, 1))) for j, t in own if j == 0}
-    return stencil_substeps({(j, t): windows[j, t] for j, t in own if j < tracers}, stencils)
+        theirs = places_of(mine, behind, -d) < SUB
+        return jnp.where(theirs, rolled(received[g, t], d - SUB * q, 1), mine)
+
+    windows = {(j, t): joined(j, t, 0, own[j, t]) for j, t in own}
+    beside = {
+        (j, d, t): rolled(windows[j, t], d, 1) if own_moved is None else joined(j, t, d, own_moved[j, d, t])
+        for j, d in moved_pairs(tracers)
+        for t in tiles
+    }
+    stencils = {
+        t: stencil(
+            *(windows[tracers + j, t] for j in (2, 3, 0, 1)), [beside[j, d, t] for j, d in moved_pairs(tracers)[2 * tracers :]]
+        )
+        for t in tiles
+    }
+    contents = {(j, t): windows[j, t] for j, t in own if j < tracers}
+    return stencil_substeps(contents, stencils, {(q, d): beside[q[0], d, q[1]] for q in contents for d in (-1, 1)})
 
 
 def pack_kernel(
@@ -197,16 +221,29 @@
 
 
 def side_kernel(
-    wet, vertical, mixing_vertical,
-    down, up, from_first, from_last, pivots, ratios, couplings, weights, rims,
+    wet, vertical, mixing_vertical, west_tiles, east_tiles,
+    far_tiles, far_moved, down, up, from_first, from_last, pivots, ratios, couplings, weights, rims,
 ):
+    arrays, tiles = east_tiles.shape[:2]
+    even = lax.axis_index("gx") % 2 == 0
+    own = {
+        (j, t): jnp.where(even, west_tiles[j, t], east_tiles[j, t]) for j in range(arrays) for t in range(tiles)
+    }
+    moved = {
+        (n, t): rolled(own[j, t], d, 1) for n, (j, d) in enumerate(moved_pairs(arrays - 4)) for t in range(tiles)
+    }
     vertical_statics(
         wet, vertical, mixing_vertical, down, up, from_first, from_last, pivots, ratios, couplings, weights, rims
     )
+    for j, t in own:
+        far_tiles[j, t] = own[j, t]
+    for n, t in moved:
+        far_moved[n, t] = moved[n, t]
 
 
 def interior_kernel(
-    tracer, mixing, east, north, wet, weights, west_tiles, east_tiles, near, lateral, sums, near_edges, far_tiles
+    tracer, mixing, east, north, wet, weights, west_tiles, east_tiles, near,
+    lateral, sums, near_edges,
 ):
     levels = wet.shape[0]
     tracers = tracer.shape[0]
@@ -216,7 +253,6 @@
     for j in range(arrays):
         for t in range(tiles):
             own[j, t] = jnp.where(even, east_tiles[j, t], west_tiles[j, t])
-            far_tiles[j, t] = jnp.where(even, west_tiles[j, t], east_tiles[j, t])
     done = window_results(own, received, even, tracers)
     coefficients = {k: lateral_coefficients(east[k], north[k], mixing[k], wet[k]) for k in range(levels)}
     planes = {(i, k): tracer[i, k] for k in range(levels) for i in range(tracers)}
@@ -286,7 +322,7 @@
         rims[n] = value
 
 
-def rim_kernel(far_tiles, far, near_edges, lateral, weights, sums, rims, edges, message):
+def rim_kernel(far_tiles, far_moved, far, near_edges, lateral, weights, sums, rims, edges, message):
     tracers, levels, _, width = lateral.shape
     odd = lax.axis_index("gx") % 2 == 1
     slots = slots_of(levels, width)
@@ -294,7 +330,8 @@
     lanes = lanes_of(rims[0])
     own = {(j, t): far_tiles[j, t] for j in range(arrays) for t in range(tiles)}
     received = {(g, t): far[g, t] for g in range(far.shape[0]) for t in range(tiles)}
-    done = window_results(own, received, odd, tracers)
+    moved = {(j, d, t): far_moved[n, t] for n, (j, d) in enumerate(moved_pairs(tracers)) for t in range(tiles)}
+    done = window_results(own, received, odd, tracers, moved)
     from_far = places_of(rims[0], jnp.logical_not(odd)) < SUB
     edge = {(i, t): jnp.where(from_far, done[i, t], near_edges[i, t]) for i, t in done}
     at_rim = rim_lanes(lanes)
@@ -448,15 +485,17 @@
     )
     far = lax.ppermute(to_far, "gx", far_pairs)
     near = lax.ppermute(to_near, "gx", near_pairs)
-    down, up, from_first, from_last, pivots, ratios, couplings, weights, rims = call(
+    far_tiles, far_moved, down, up, from_first, from_last, pivots, ratios, couplings, weights, rims = call(
         side_kernel,
-        [block] * 7 + [(2,) + block, (5,) + plane],
+        [(arrays, tiles) + plane, (len(moved_pairs(tracers)), tiles) + plane]
+        + [block] * 7
+        + [(2,) + block, (5,) + plane],
         50 * cells,
-        wet, vertical, mixing_down,
-    )
-    lateral, sums, near_edges, far_tiles = call(
+        wet, vertical, mixing_down, west_tiles, east_tiles,
+    )
+    lateral, sums, near_edges = call(
         interior_kernel,
-        [tracer.shape, (2 * tracers,) + plane, (tracers, tiles) + plane, (arrays, tiles) + plane],
+        [tracer.shape, (2 * tracers,) + plane, (tracers, tiles) + plane],
         100 * cells,
         tracer_here, mixing, east, north, wet, weights, west_tiles, east_tiles, near,
     )
@@ -464,7 +503,7 @@
         rim_kernel,
         [(tracers, tiles) + plane, (3 * tracers + 4,) + plane],
         20 * cells,
-        far_tiles, far, near_edges, lateral, weights, sums, rims,
+        far_tiles, far_moved, far, near_edges, lateral, weights, sums, rims,
     )
     other = lax.ppermute(message, "gz", [(i, i ^ 1) for i in range(4)])
     merged, kept = call(

time: 18.3 us -> 18.3 us (level)
  no operation moved by 1% of the time
where the time goes in v4:
time: 18.3 us; the launch traced here: 18.2 us
  starting transfers between devices  8.69 us (47%)
  Pallas kernels  4.81 us (26%)
  waiting for transfers between devices  4.63 us (25%)
    pallas_call x7, Pallas kernels, call(): pl.pallas_call(kernel, out_shape=outs, in_specs=in_specs or [VMEM] * len(...  4.81 us
    ppermute x1, starting transfers between devices, local(): far = lax.ppermute(to_far, 'gx', far_pairs)  3.56 us
    ppermute x1, starting transfers between devices, local(): beyond = lax.ppermute(merged, 'gz', [(i, i ^ 2) for i in range(4)])  2.81 us
    ppermute x1, waiting for transfers between devices, local(): other = lax.ppermute(message, 'gz', [(i, i ^ 1) for i in range(4)])  2.71 us
    ppermute x1, starting transfers between devices, local(): other = lax.ppermute(message, 'gz', [(i, i ^ 1) for i in range(4)])  1.8 us
    ppermute x1, waiting for transfers between devices, local(): beyond = lax.ppermute(merged, 'gz', [(i, i ^ 2) for i in range(4)])  1.8 us
    ppermute x1, starting transfers between devices, local(): near = lax.ppermute(to_near, 'gx', near_pairs)  0.52 us
  transfers between devices with their start and end apart: 4, of which 3 were waited for; matrix products, arithmetic and copies ran while one was open for 0% of the time, Pallas kernels for 10%

profile of v4, /device:TPU:0, one launch (start us, length us, event | category | flops | bytes accessed | tf_op | source)
XLA Modules:
  0.0 18.2 jit_solution(12370425419464136670)
XLA Ops:
  0.0 1.7 %shard_map.82 = (f32[2,25,16,128]{3,2,1,0:T(8,128)S(1)}, f32[25,16,128]{2,1,0:T(8,128)S(1)}, f32[25,16,128]{2,1,0:T(8,128)S(1)}, f32[25,16,128]{2,1,0:T(8,128)S(...) custom-call(f32[2,25,16,128]{3,2,1,0:T(8,128)} %tracer_in.1, ...), custom_call_target="tpu_custom_call" | custom-call | flops 1024000 | bytes 3547136 | tf_op jit(solution)/shard_map/pallas_call | solution.py:21
  1.7 0.5 %collective-permute-start.1 = (f32[2,2,16,128]{3,2,1,0:T(8,128)S(1)}, f32[2,2,16,128]{3,2,1,0:T(8,128)S(1)}, u32[]{:S(2)}, u32[]{:S(2)}) collective-permute-start(f32[2,2,16,128]{3,2,1,0:T(8,128)S(1)} %get-tuple-element.49), channel_id=1, source_target_pairs={{0,4},{4,0},{8,12},{12,8},{16,20},{20,16},{24,28},{28,24},{1,5},{5... | collective-permute-start | bytes 98312 | tf_op jit(solution)/shard_map/ppermute | solution.py:487
  2.2 3.6 %collective-permute-start = (f32[2,2,16,128]{3,2,1,0:T(8,128)S(1)}, f32[2,2,16,128]{3,2,1,0:T(8,128)S(1)}, u32[]{:S(2)}, u32[]{:S(2)}) collective-permute-start(f32[2,2,16,128]{3,2,1,0:T(8,128)S(1)} %get-tuple-element.43), channel_id=1, source_target_pairs={{0,28},{4,8},{8,4},{12,16},{16,12},{20,24},{24,20},{28,0},{1,29},{... | collective-permute-start | bytes 98312 | tf_op jit(solution)/shard_map/ppermute | solution.py:486
  5.8 0.3 %shard_map.83 = (f32[6,2,16,128]{3,2,1,0:T(8,128)S(1)}, f32[9,2,16,128]{3,2,1,0:T(8,128)S(1)}, f32[25,16,128]{2,1,0:T(8,128)S(1)}, f32[25,16,128]{2,1,0:T(8,128)...) custom-call(f32[25,16,128]{2,1,0:T(8,128)S(1)} %get-tuple-element.36, ...), custom_call_target="tpu_custom_call" | custom-call | flops 2560000 | bytes 2940928 | tf_op jit(solution)/shard_map/pallas_call | solution.py:21
  6.1 0.0 collective-permute-done.1.near
  6.1 1.2 %shard_map.84 = (f32[2,25,16,128]{3,2,1,0:T(8,128)S(1)}, f32[4,16,128]{2,1,0:T(8,128)S(1)}, f32[2,2,16,128]{3,2,1,0:T(8,128)S(1)}) custom-call(f32[2,25,16,128]{3,2,1,0:T(8,128)S(1)} %get-tuple-element.44.tracer, f32[25,16,128]{2,1,0:T(8,128)S(1)} %get-tuple-element.45.mixing, f32[25,16,128]{2,1,0:T(8,128)S(1)} %get-tuple-element.46.east, ...), custom_call_target="tpu_custom_call" | custom-call | flops 5120000 | bytes 2342912 | tf_op jit(solution)/shard_map/pallas_call | solution.py:21
  7.3 0.1 collective-permute-done.far
  7.4 0.5 %shard_map.85 = (f32[2,2,16,128]{3,2,1,0:T(8,128)S(1)}, f32[10,16,128]{2,1,0:T(8,128)S(1)}) custom-call(f32[6,2,16,128]{3,2,1,0:T(8,128)S(1)} %get-tuple-element.41.far_tiles, f32[9,2,16,128]{3,2,1,0:T(8,128)S(1)} %get-tuple-element.42.far_moved, f32[2,2,16,128]{3,2,1,0:T(8,128)S(1)} %collective-permute-done.far, ...), custom_call_target="tpu_custom_call" | custom-call | flops 1024000 | bytes 1318912 | tf_op jit(solution)/shard_map/pallas_call | solution.py:21
  7.9 1.8 %collective-permute-start.2 = (f32[10,16,128]{2,1,0:T(8,128)S(1)}, f32[10,16,128]{2,1,0:T(8,128)S(1)}, u32[]{:S(2)}, u32[]{:S(2)}) collective-permute-start(f32[10,16,128]{2,1,0:T(8,128)S(1)} %get-tuple-element.54.own), channel_id=1, source_target_pairs={{0,1},{1,0},{2,3},{3,2},{4,5},{5,4},{6,7},{7,6},{8,9},{9,8},{10,11... | collective-permute-start | bytes 245768 | tf_op jit(solution)/shard_map/ppermute | solution.py:508
  9.7 2.7 %collective-permute-done.2.other = f32[10,16,128]{2,1,0:T(8,128)S(1)} collective-permute-done((f32[10,16,128]{2,1,0:T(8,128)S(1)}, f32[10,16,128]{2,1,0:T(8,128)S(1)}, u32[]{:S(2)}, u32[]{:S(2)}) %collective-permute-start.2) | collective-permute-done | bytes 81952 | tf_op jit(solution)/shard_map/ppermute | solution.py:508
  12.4 2.8 %collective-permute-start.3 = (f32[5,16,128]{2,1,0:T(8,128)S(1)}, f32[5,16,128]{2,1,0:T(8,128)S(1)}, u32[]{:S(2)}, u32[]{:S(2)}) collective-permute-start(f32[5,16,128]{2,1,0:T(8,128)S(1)} %get-tuple-element.55.own), channel_id=1, source_target_pairs={{0,2},{1,3},{2,0},{3,1},{4,6},{5,7},{6,4},{7,5},{8,10},{9,11},{10,... | collective-permute-start | bytes 122888 | tf_op jit(solution)/shard_map/ppermute | solution.py:512
  15.2 0.4 %shard_map.87 = (f32[2,25,16,128]{3,2,1,0:T(8,128)S(1)}, f32[25,16,128]{2,1,0:T(8,128)S(1)}) custom-call(f32[2,25,16,128]{3,2,1,0:T(8,128)S(1)} %get-tuple-element.51.lateral, f32[2,2,16,128]{3,2,1,0:T(8,128)S(1)} %get-tuple-element.56.edges, f32[25,16,128]{2,1,0:T(8,128)S(1)} %get-tuple-element.57.down, f32[25,16,128]{2,1,0:T(8,128)S(1)} %get-tuple-element.58.up, ...), custom_call_target="tpu_custom_call" | custom-call | flops 2048000 | bytes 2514944 | tf_op jit(solution)/shard_map/pallas_call | solution.py:21
  15.6 1.8 %collective-permute-done.3.other = f32[5,16,128]{2,1,0:T(8,128)S(1)} collective-permute-done((f32[5,16,128]{2,1,0:T(8,128)S(1)}, f32[5,16,128]{2,1,0:T(8,128)S(1)}, u32[]{:S(2)}, u32[]{:S(2)}) %collective-permute-start.3) | collective-permute-done | bytes 40992 | tf_op jit(solution)/shard_map/ppermute | solution.py:512
  17.4 0.8 %shard_map.88 = f32[2,25,16,128]{3,2,1,0:T(8,128)} custom-call(f32[5,16,128]{2,1,0:T(8,128)S(1)} %get-tuple-element.55.own, f32[5,16,128]{2,1,0:T(8,128)S(1)} %collective-permute-done.3.other, f32[2,25,16,128]{3,2,1,0:T(8,128)S(1)} %get-tuple-element.65.base, f32[25,16,128]{2,1,0:T(8,128)S(1)} %get-tuple-element.66.gain), custom_call_target="tpu_custom_call" | custom-call | flops 512000 | bytes 1105920 | tf_op jit(solution)/shard_map/pallas_call | solution.py:21
  (1 shorter events, 0.0 us)
Async XLA Ops:
  1.7 4.4 %collective-permute-start.1 = (f32[2,2,16,128]{3,2,1,0:T(8,128)S(1)}, f32[2,2,16,128]{3,2,1,0:T(8,128)S(1)}, u32[]{:S(2)}, u32[]{:S(2)}) collective-permute-start(f32[2,2,16,128]{3,2,1,0:T(8,128)S(1)} %get-tuple-element.49), channel_id=1, source_target_pairs={{0,4},{4,0},{8,12},{12,8},{16,20},{20,16},{24,28},{28,24},{1,5},{5... | collective-permute-start | bytes 98312 | tf_op jit(solution)/shard_map/ppermute | solution.py:487
  2.2 5.2 %collective-permute-start = (f32[2,2,16,128]{3,2,1,0:T(8,128)S(1)}, f32[2,2,16,128]{3,2,1,0:T(8,128)S(1)}, u32[]{:S(2)}, u32[]{:S(2)}) collective-permute-start(f32[2,2,16,128]{3,2,1,0:T(8,128)S(1)} %get-tuple-element.43), channel_id=1, source_target_pairs={{0,28},{4,8},{8,4},{12,16},{16,12},{20,24},{24,20},{28,0},{1,29},{... | collective-permute-start | bytes 98312 | tf_op jit(solution)/shard_map/ppermute | solution.py:486
  7.9 4.5 %collective-permute-start.2 = (f32[10,16,128]{2,1,0:T(8,128)S(1)}, f32[10,16,128]{2,1,0:T(8,128)S(1)}, u32[]{:S(2)}, u32[]{:S(2)}) collective-permute-start(f32[10,16,128]{2,1,0:T(8,128)S(1)} %get-tuple-element.54.own), channel_id=1, source_target_pairs={{0,1},{1,0},{2,3},{3,2},{4,5},{5,4},{6,7},{7,6},{8,9},{9,8},{10,11... | collective-permute-start | bytes 245768 | tf_op jit(solution)/shard_map/ppermute | solution.py:508
  12.4 5.0 %collective-permute-start.3 = (f32[5,16,128]{2,1,0:T(8,128)S(1)}, f32[5,16,128]{2,1,0:T(8,128)S(1)}, u32[]{:S(2)}, u32[]{:S(2)}) collective-permute-start(f32[5,16,128]{2,1,0:T(8,128)S(1)} %get-tuple-element.55.own), channel_id=1, source_target_pairs={{0,2},{1,3},{2,0},{3,1},{4,6},{5,7},{6,4},{7,5},{8,10},{9,11},{10,... | collective-permute-start | bytes 122888 | tf_op jit(solution)/shard_map/ppermute | solution.py:512

commit v5 on v4

--- a/solution.py
+++ b/solution.py
@@ -178,12 +178,13 @@
 ):
     levels, _, width = mask.shape
     tracers = tracer.shape[0]
-    pairs = [(tracer_in.at[i], tracer.at[i]) for i in range(tracers)]
-    pairs += [(east_in, east), (bottom_in, bottom), (mask_in, mask), (north_in, north), (mixing_in, mixing)]
-    pairs += [(vertical_in, vertical), (mixing_vertical_in, mixing_vertical)]
-    copies = [pltpu.make_async_copy(source, target, sems.at[n]) for n, (source, target) in enumerate(pairs)]
+    assert tracers == 2
+    pairs = [(tracer_in, tracer, 0), (east_in, east, 1), (bottom_in, bottom, 2), (mask_in, mask, 3), (north_in, north, 3)]
+    pairs += [(mixing_in, mixing, 4), (vertical_in, vertical, 5), (mixing_vertical_in, mixing_vertical, 5)]
+    copies = [pltpu.make_async_copy(source, target, sems.at[n]) for source, target, n in pairs]
     for copy in copies:
         copy.start()
+    two_blocks = [pltpu.make_async_copy(tracer_in, tracer, sems.at[n]) for n in (3, 5)]
     slots = slots_of(levels, width)
     even = lax.axis_index("gx") % 2 == 0
     found = {}
@@ -192,14 +193,15 @@
         found[j, t] = pair[0]
         west_tiles[j, t], east_tiles[j, t] = pair
 
-    for copy in copies[: tracers + 1]:
-        copy.wait()
+    copies[0].wait()
+    copies[1].wait()
     for t, part in enumerate(slots):
         for i in range(tracers):
             find(i, t, window_tiles(lambda k: tracer[i, k], part))
         find(tracers + 2, t, window_tiles(lambda k: east[k], part))
-    for copy in copies[tracers + 1 : -2]:
-        copy.wait()
+    copies[2].wait()
+    two_blocks[0].wait()
+    copies[5].wait()
     floor = bottom[...] - lax.axis_index("gz") * levels
     signed = []
     for k in range(levels):
@@ -216,8 +218,7 @@
             group = [found[g * GROUP + q, t] for q in range(GROUP)]
             to_far[g, t] = pack_group(group, even)
             to_near[g, t] = pack_group(group, jnp.logical_not(even))
-    for copy in copies[-2:]:
-        copy.wait()
+    two_blocks[1].wait()
 
 
 def side_kernel(
@@ -441,20 +442,17 @@
         )
 
 
-def final_kernel(own, other, base, gain, out, staged, sems):
+def final_kernel(own, other, base, gain, out, staged, sem):
     tracers, levels = base.shape[:2]
     lower_pair = lax.axis_index("gz") >= 2
     upper = [jnp.where(lower_pair, other[j], own[j]) for j in range(own.shape[0])]
     lower = [jnp.where(lower_pair, own[j], other[j]) for j in range(own.shape[0])]
     middle, _ = interface(upper[: tracers + 2], lower, tracers)
-    copies = []
     for i in range(tracers):
         for k in range(levels):
             staged[i, k] = base[i, k] + middle[i] * gain[k]
-        copies.append(pltpu.make_async_copy(staged.at[i], out.at[i], sems.at[i]))
-        copies[i].start()
-    for copy in copies:
-        copy.wait()
+        pltpu.make_async_copy(staged.at[i], out.at[i], sem).start()
+    pltpu.make_async_copy(staged, out, sem).wait()
 
 
 def local(
@@ -480,7 +478,7 @@
         scratch=[
             pltpu.VMEM(block, jnp.int32),
             pltpu.VMEM(plane, jnp.int32),
-            pltpu.SemaphoreType.DMA((tracers + 7,)),
+            pltpu.SemaphoreType.DMA((6,)),
         ],
     )
     far = lax.ppermute(to_far, "gx", far_pairs)
@@ -519,7 +517,7 @@
     (result,) = call(
         final_kernel, [tracer.shape], 10 * cells, merged, beyond, base, gain,
         out_specs=[HBM],
-        scratch=[pltpu.VMEM(tracer.shape, jnp.float32), pltpu.SemaphoreType.DMA((tracers,))],
+        scratch=[pltpu.VMEM(tracer.shape, jnp.float32), pltpu.SemaphoreType.DMA],
     )
     return result
 

time: 18.3 us -> 18.2 us (level)
  no operation moved by 1% of the time
where the time goes in v5:
time: 18.2 us; the launch traced here: 18 us
  starting transfers between devices  8.69 us (48%)
  Pallas kernels  4.69 us (26%)
  waiting for transfers between devices  4.63 us (25%)
    pallas_call x7, Pallas kernels, call(): pl.pallas_call(kernel, out_shape=outs, in_specs=in_specs or [VMEM] * len(...  4.69 us
    ppermute x1, starting transfers between devices, local(): far = lax.ppermute(to_far, 'gx', far_pairs)  3.56 us
    ppermute x1, starting transfers between devices, local(): beyond = lax.ppermute(merged, 'gz', [(i, i ^ 2) for i in range(4)])  2.81 us
    ppermute x1, waiting for transfers between devices, local(): other = lax.ppermute(message, 'gz', [(i, i ^ 1) for i in range(4)])  2.71 us
    ppermute x1, starting transfers between devices, local(): other = lax.ppermute(message, 'gz', [(i, i ^ 1) for i in range(4)])  1.8 us
    ppermute x1, waiting for transfers between devices, local(): beyond = lax.ppermute(merged, 'gz', [(i, i ^ 2) for i in range(4)])  1.8 us
    ppermute x1, starting transfers between devices, local(): near = lax.ppermute(to_near, 'gx', near_pairs)  0.52 us
  transfers between devices with their start and end apart: 4, of which 3 were waited for; matrix products, arithmetic and copies ran while one was open for 0% of the time, Pallas kernels for 10%

profile of v5, /device:TPU:0, one launch (start us, length us, event | category | flops | bytes accessed | tf_op | source)
XLA Modules:
  0.0 18.0 jit_solution(13675509393775191865)
XLA Ops:
  0.0 1.6 %shard_map.82 = (f32[2,25,16,128]{3,2,1,0:T(8,128)S(1)}, f32[25,16,128]{2,1,0:T(8,128)S(1)}, f32[25,16,128]{2,1,0:T(8,128)S(1)}, f32[25,16,128]{2,1,0:T(8,128)S(...) custom-call(f32[2,25,16,128]{3,2,1,0:T(8,128)} %tracer_in.1, ...), custom_call_target="tpu_custom_call" | custom-call | flops 1024000 | bytes 3547136 | tf_op jit(solution)/shard_map/pallas_call | solution.py:21
  1.6 0.5 %collective-permute-start.1 = (f32[2,2,16,128]{3,2,1,0:T(8,128)S(1)}, f32[2,2,16,128]{3,2,1,0:T(8,128)S(1)}, u32[]{:S(2)}, u32[]{:S(2)}) collective-permute-start(f32[2,2,16,128]{3,2,1,0:T(8,128)S(1)} %get-tuple-element.49), channel_id=1, source_target_pairs={{0,4},{4,0},{8,12},{12,8},{16,20},{20,16},{24,28},{28,24},{1,5},{5... | collective-permute-start | bytes 98312 | tf_op jit(solution)/shard_map/ppermute | solution.py:485
  2.1 3.6 %collective-permute-start = (f32[2,2,16,128]{3,2,1,0:T(8,128)S(1)}, f32[2,2,16,128]{3,2,1,0:T(8,128)S(1)}, u32[]{:S(2)}, u32[]{:S(2)}) collective-permute-start(f32[2,2,16,128]{3,2,1,0:T(8,128)S(1)} %get-tuple-element.43), channel_id=1, source_target_pairs={{0,28},{4,8},{8,4},{12,16},{16,12},{20,24},{24,20},{28,0},{1,29},{... | collective-permute-start | bytes 98312 | tf_op jit(solution)/shard_map/ppermute | solution.py:484
  5.7 0.3 %shard_map.83 = (f32[6,2,16,128]{3,2,1,0:T(8,128)S(1)}, f32[9,2,16,128]{3,2,1,0:T(8,128)S(1)}, f32[25,16,128]{2,1,0:T(8,128)S(1)}, f32[25,16,128]{2,1,0:T(8,128)...) custom-call(f32[25,16,128]{2,1,0:T(8,128)S(1)} %get-tuple-element.36, ...), custom_call_target="tpu_custom_call" | custom-call | flops 2560000 | bytes 2940928 | tf_op jit(solution)/shard_map/pallas_call | solution.py:21
  6.0 0.0 collective-permute-done.1.near
  6.0 1.2 %shard_map.84 = (f32[2,25,16,128]{3,2,1,0:T(8,128)S(1)}, f32[4,16,128]{2,1,0:T(8,128)S(1)}, f32[2,2,16,128]{3,2,1,0:T(8,128)S(1)}) custom-call(f32[2,25,16,128]{3,2,1,0:T(8,128)S(1)} %get-tuple-element.44.tracer, f32[25,16,128]{2,1,0:T(8,128)S(1)} %get-tuple-element.45.mixing, f32[25,16,128]{2,1,0:T(8,128)S(1)} %get-tuple-element.46.east, ...), custom_call_target="tpu_custom_call" | custom-call | flops 5120000 | bytes 2342912 | tf_op jit(solution)/shard_map/pallas_call | solution.py:21
  7.2 0.1 collective-permute-done.far
  7.3 0.5 %shard_map.85 = (f32[2,2,16,128]{3,2,1,0:T(8,128)S(1)}, f32[10,16,128]{2,1,0:T(8,128)S(1)}) custom-call(f32[6,2,16,128]{3,2,1,0:T(8,128)S(1)} %get-tuple-element.41.far_tiles, f32[9,2,16,128]{3,2,1,0:T(8,128)S(1)} %get-tuple-element.42.far_moved, f32[2,2,16,128]{3,2,1,0:T(8,128)S(1)} %collective-permute-done.far, ...), custom_call_target="tpu_custom_call" | custom-call | flops 1024000 | bytes 1318912 | tf_op jit(solution)/shard_map/pallas_call | solution.py:21
  7.7 1.8 %collective-permute-start.2 = (f32[10,16,128]{2,1,0:T(8,128)S(1)}, f32[10,16,128]{2,1,0:T(8,128)S(1)}, u32[]{:S(2)}, u32[]{:S(2)}) collective-permute-start(f32[10,16,128]{2,1,0:T(8,128)S(1)} %get-tuple-element.54.own), channel_id=1, source_target_pairs={{0,1},{1,0},{2,3},{3,2},{4,5},{5,4},{6,7},{7,6},{8,9},{9,8},{10,11... | collective-permute-start | bytes 245768 | tf_op jit(solution)/shard_map/ppermute | solution.py:506
  9.5 2.7 %collective-permute-done.2.other = f32[10,16,128]{2,1,0:T(8,128)S(1)} collective-permute-done((f32[10,16,128]{2,1,0:T(8,128)S(1)}, f32[10,16,128]{2,1,0:T(8,128)S(1)}, u32[]{:S(2)}, u32[]{:S(2)}) %collective-permute-start.2) | collective-permute-done | bytes 81952 | tf_op jit(solution)/shard_map/ppermute | solution.py:506
  12.3 2.8 %collective-permute-start.3 = (f32[5,16,128]{2,1,0:T(8,128)S(1)}, f32[5,16,128]{2,1,0:T(8,128)S(1)}, u32[]{:S(2)}, u32[]{:S(2)}) collective-permute-start(f32[5,16,128]{2,1,0:T(8,128)S(1)} %get-tuple-element.55.own), channel_id=1, source_target_pairs={{0,2},{1,3},{2,0},{3,1},{4,6},{5,7},{6,4},{7,5},{8,10},{9,11},{10,... | collective-permute-start | bytes 122888 | tf_op jit(solution)/shard_map/ppermute | solution.py:510
  15.1 0.4 %shard_map.87 = (f32[2,25,16,128]{3,2,1,0:T(8,128)S(1)}, f32[25,16,128]{2,1,0:T(8,128)S(1)}) custom-call(f32[2,25,16,128]{3,2,1,0:T(8,128)S(1)} %get-tuple-element.51.lateral, f32[2,2,16,128]{3,2,1,0:T(8,128)S(1)} %get-tuple-element.56.edges, f32[25,16,128]{2,1,0:T(8,128)S(1)} %get-tuple-element.57.down, f32[25,16,128]{2,1,0:T(8,128)S(1)} %get-tuple-element.58.up, ...), custom_call_target="tpu_custom_call" | custom-call | flops 2048000 | bytes 2514944 | tf_op jit(solution)/shard_map/pallas_call | solution.py:21
  15.5 1.8 %collective-permute-done.3.other = f32[5,16,128]{2,1,0:T(8,128)S(1)} collective-permute-done((f32[5,16,128]{2,1,0:T(8,128)S(1)}, f32[5,16,128]{2,1,0:T(8,128)S(1)}, u32[]{:S(2)}, u32[]{:S(2)}) %collective-permute-start.3) | collective-permute-done | bytes 40992 | tf_op jit(solution)/shard_map/ppermute | solution.py:510
  17.3 0.8 %shard_map.88 = f32[2,25,16,128]{3,2,1,0:T(8,128)} custom-call(f32[5,16,128]{2,1,0:T(8,128)S(1)} %get-tuple-element.55.own, f32[5,16,128]{2,1,0:T(8,128)S(1)} %collective-permute-done.3.other, f32[2,25,16,128]{3,2,1,0:T(8,128)S(1)} %get-tuple-element.65.base, f32[25,16,128]{2,1,0:T(8,128)S(1)} %get-tuple-element.66.gain), custom_call_target="tpu_custom_call" | custom-call | flops 512000 | bytes 1105920 | tf_op jit(solution)/shard_map/pallas_call | solution.py:21
  (1 shorter events, 0.0 us)
Async XLA Ops:
  1.6 4.4 %collective-permute-start.1 = (f32[2,2,16,128]{3,2,1,0:T(8,128)S(1)}, f32[2,2,16,128]{3,2,1,0:T(8,128)S(1)}, u32[]{:S(2)}, u32[]{:S(2)}) collective-permute-start(f32[2,2,16,128]{3,2,1,0:T(8,128)S(1)} %get-tuple-element.49), channel_id=1, source_target_pairs={{0,4},{4,0},{8,12},{12,8},{16,20},{20,16},{24,28},{28,24},{1,5},{5... | collective-permute-start | bytes 98312 | tf_op jit(solution)/shard_map/ppermute | solution.py:485
  2.1 5.2 %collective-permute-start = (f32[2,2,16,128]{3,2,1,0:T(8,128)S(1)}, f32[2,2,16,128]{3,2,1,0:T(8,128)S(1)}, u32[]{:S(2)}, u32[]{:S(2)}) collective-permute-start(f32[2,2,16,128]{3,2,1,0:T(8,128)S(1)} %get-tuple-element.43), channel_id=1, source_target_pairs={{0,28},{4,8},{8,4},{12,16},{16,12},{20,24},{24,20},{28,0},{1,29},{... | collective-permute-start | bytes 98312 | tf_op jit(solution)/shard_map/ppermute | solution.py:484
  7.7 4.5 %collective-permute-start.2 = (f32[10,16,128]{2,1,0:T(8,128)S(1)}, f32[10,16,128]{2,1,0:T(8,128)S(1)}, u32[]{:S(2)}, u32[]{:S(2)}) collective-permute-start(f32[10,16,128]{2,1,0:T(8,128)S(1)} %get-tuple-element.54.own), channel_id=1, source_target_pairs={{0,1},{1,0},{2,3},{3,2},{4,5},{5,4},{6,7},{7,6},{8,9},{9,8},{10,11... | collective-permute-start | bytes 245768 | tf_op jit(solution)/shard_map/ppermute | solution.py:506
  12.3 5.0 %collective-permute-start.3 = (f32[5,16,128]{2,1,0:T(8,128)S(1)}, f32[5,16,128]{2,1,0:T(8,128)S(1)}, u32[]{:S(2)}, u32[]{:S(2)}) collective-permute-start(f32[5,16,128]{2,1,0:T(8,128)S(1)} %get-tuple-element.55.own), channel_id=1, source_target_pairs={{0,2},{1,3},{2,0},{3,1},{4,6},{5,7},{6,4},{7,5},{8,10},{9,11},{10,... | collective-permute-start | bytes 122888 | tf_op jit(solution)/shard_map/ppermute | solution.py:510

commit v6 on v5

--- a/solution.py
+++ b/solution.py
@@ -179,8 +179,8 @@
     levels, _, width = mask.shape
     tracers = tracer.shape[0]
     assert tracers == 2
-    pairs = [(tracer_in, tracer, 0), (east_in, east, 1), (bottom_in, bottom, 2), (mask_in, mask, 3), (north_in, north, 3)]
-    pairs += [(mixing_in, mixing, 4), (vertical_in, vertical, 5), (mixing_vertical_in, mixing_vertical, 5)]
+    pairs = [(tracer_in, tracer, 0), (east_in, east, 1), (bottom_in, bottom, 2), (mask_in, mask, 3), (mixing_in, mixing, 3)]
+    pairs += [(north_in, north, 4), (vertical_in, vertical, 5), (mixing_vertical_in, mixing_vertical, 5)]
     copies = [pltpu.make_async_copy(source, target, sems.at[n]) for source, target, n in pairs]
     for copy in copies:
         copy.start()

time: 18.2 us -> 18.2 us (level)
  no operation moved by 1% of the time
where the time goes in v6:
time: 18.2 us; the launch traced here: 18 us
  starting transfers between devices  8.69 us (48%)
  Pallas kernels  4.69 us (26%)
  waiting for transfers between devices  4.63 us (25%)
    pallas_call x7, Pallas kernels, call(): pl.pallas_call(kernel, out_shape=outs, in_specs=in_specs or [VMEM] * len(...  4.69 us
    ppermute x1, starting transfers between devices, local(): far = lax.ppermute(to_far, 'gx', far_pairs)  3.56 us
    ppermute x1, starting transfers between devices, local(): beyond = lax.ppermute(merged, 'gz', [(i, i ^ 2) for i in range(4)])  2.81 us
    ppermute x1, waiting for transfers between devices, local(): other = lax.ppermute(message, 'gz', [(i, i ^ 1) for i in range(4)])  2.71 us
    ppermute x1, starting transfers between devices, local(): other = lax.ppermute(message, 'gz', [(i, i ^ 1) for i in range(4)])  1.8 us
    ppermute x1, waiting for transfers between devices, local(): beyond = lax.ppermute(merged, 'gz', [(i, i ^ 2) for i in range(4)])  1.8 us
    ppermute x1, starting transfers between devices, local(): near = lax.ppermute(to_near, 'gx', near_pairs)  0.52 us
  transfers between devices with their start and end apart: 4, of which 3 were waited for; matrix products, arithmetic and copies ran while one was open for 0% of the time, Pallas kernels for 10%

profile of v6, /device:TPU:0, one launch (start us, length us, event | category | flops | bytes accessed | tf_op | source)
XLA Modules:
  0.0 18.0 jit_solution(11375379354690104096)
XLA Ops:
  0.0 1.6 %shard_map.82 = (f32[2,25,16,128]{3,2,1,0:T(8,128)S(1)}, f32[25,16,128]{2,1,0:T(8,128)S(1)}, f32[25,16,128]{2,1,0:T(8,128)S(1)}, f32[25,16,128]{2,1,0:T(8,128)S(...) custom-call(f32[2,25,16,128]{3,2,1,0:T(8,128)} %tracer_in.1, ...), custom_call_target="tpu_custom_call" | custom-call | flops 1024000 | bytes 3547136 | tf_op jit(solution)/shard_map/pallas_call | solution.py:21
  1.6 0.5 %collective-permute-start.1 = (f32[2,2,16,128]{3,2,1,0:T(8,128)S(1)}, f32[2,2,16,128]{3,2,1,0:T(8,128)S(1)}, u32[]{:S(2)}, u32[]{:S(2)}) collective-permute-start(f32[2,2,16,128]{3,2,1,0:T(8,128)S(1)} %get-tuple-element.49), channel_id=1, source_target_pairs={{0,4},{4,0},{8,12},{12,8},{16,20},{20,16},{24,28},{28,24},{1,5},{5... | collective-permute-start | bytes 98312 | tf_op jit(solution)/shard_map/ppermute | solution.py:485
  2.1 3.6 %collective-permute-start = (f32[2,2,16,128]{3,2,1,0:T(8,128)S(1)}, f32[2,2,16,128]{3,2,1,0:T(8,128)S(1)}, u32[]{:S(2)}, u32[]{:S(2)}) collective-permute-start(f32[2,2,16,128]{3,2,1,0:T(8,128)S(1)} %get-tuple-element.43), channel_id=1, source_target_pairs={{0,28},{4,8},{8,4},{12,16},{16,12},{20,24},{24,20},{28,0},{1,29},{... | collective-permute-start | bytes 98312 | tf_op jit(solution)/shard_map/ppermute | solution.py:484
  5.7 0.3 %shard_map.83 = (f32[6,2,16,128]{3,2,1,0:T(8,128)S(1)}, f32[9,2,16,128]{3,2,1,0:T(8,128)S(1)}, f32[25,16,128]{2,1,0:T(8,128)S(1)}, f32[25,16,128]{2,1,0:T(8,128)...) custom-call(f32[25,16,128]{2,1,0:T(8,128)S(1)} %get-tuple-element.36, ...), custom_call_target="tpu_custom_call" | custom-call | flops 2560000 | bytes 2940928 | tf_op jit(solution)/shard_map/pallas_call | solution.py:21
  6.0 0.0 collective-permute-done.1.near
  6.0 1.2 %shard_map.84 = (f32[2,25,16,128]{3,2,1,0:T(8,128)S(1)}, f32[4,16,128]{2,1,0:T(8,128)S(1)}, f32[2,2,16,128]{3,2,1,0:T(8,128)S(1)}) custom-call(f32[2,25,16,128]{3,2,1,0:T(8,128)S(1)} %get-tuple-element.44.tracer, f32[25,16,128]{2,1,0:T(8,128)S(1)} %get-tuple-element.45.mixing, f32[25,16,128]{2,1,0:T(8,128)S(1)} %get-tuple-element.46.east, ...), custom_call_target="tpu_custom_call" | custom-call | flops 5120000 | bytes 2342912 | tf_op jit(solution)/shard_map/pallas_call | solution.py:21
  7.2 0.1 collective-permute-done.far
  7.3 0.5 %shard_map.85 = (f32[2,2,16,128]{3,2,1,0:T(8,128)S(1)}, f32[10,16,128]{2,1,0:T(8,128)S(1)}) custom-call(f32[6,2,16,128]{3,2,1,0:T(8,128)S(1)} %get-tuple-element.41.far_tiles, f32[9,2,16,128]{3,2,1,0:T(8,128)S(1)} %get-tuple-element.42.far_moved, f32[2,2,16,128]{3,2,1,0:T(8,128)S(1)} %collective-permute-done.far, ...), custom_call_target="tpu_custom_call" | custom-call | flops 1024000 | bytes 1318912 | tf_op jit(solution)/shard_map/pallas_call | solution.py:21
  7.7 1.8 %collective-permute-start.2 = (f32[10,16,128]{2,1,0:T(8,128)S(1)}, f32[10,16,128]{2,1,0:T(8,128)S(1)}, u32[]{:S(2)}, u32[]{:S(2)}) collective-permute-start(f32[10,16,128]{2,1,0:T(8,128)S(1)} %get-tuple-element.54.own), channel_id=1, source_target_pairs={{0,1},{1,0},{2,3},{3,2},{4,5},{5,4},{6,7},{7,6},{8,9},{9,8},{10,11... | collective-permute-start | bytes 245768 | tf_op jit(solution)/shard_map/ppermute | solution.py:506
  9.5 2.7 %collective-permute-done.2.other = f32[10,16,128]{2,1,0:T(8,128)S(1)} collective-permute-done((f32[10,16,128]{2,1,0:T(8,128)S(1)}, f32[10,16,128]{2,1,0:T(8,128)S(1)}, u32[]{:S(2)}, u32[]{:S(2)}) %collective-permute-start.2) | collective-permute-done | bytes 81952 | tf_op jit(solution)/shard_map/ppermute | solution.py:506
  12.3 2.8 %collective-permute-start.3 = (f32[5,16,128]{2,1,0:T(8,128)S(1)}, f32[5,16,128]{2,1,0:T(8,128)S(1)}, u32[]{:S(2)}, u32[]{:S(2)}) collective-permute-start(f32[5,16,128]{2,1,0:T(8,128)S(1)} %get-tuple-element.55.own), channel_id=1, source_target_pairs={{0,2},{1,3},{2,0},{3,1},{4,6},{5,7},{6,4},{7,5},{8,10},{9,11},{10,... | collective-permute-start | bytes 122888 | tf_op jit(solution)/shard_map/ppermute | solution.py:510
  15.1 0.4 %shard_map.87 = (f32[2,25,16,128]{3,2,1,0:T(8,128)S(1)}, f32[25,16,128]{2,1,0:T(8,128)S(1)}) custom-call(f32[2,25,16,128]{3,2,1,0:T(8,128)S(1)} %get-tuple-element.51.lateral, f32[2,2,16,128]{3,2,1,0:T(8,128)S(1)} %get-tuple-element.56.edges, f32[25,16,128]{2,1,0:T(8,128)S(1)} %get-tuple-element.57.down, f32[25,16,128]{2,1,0:T(8,128)S(1)} %get-tuple-element.58.up, ...), custom_call_target="tpu_custom_call" | custom-call | flops 2048000 | bytes 2514944 | tf_op jit(solution)/shard_map/pallas_call | solution.py:21
  15.5 1.8 %collective-permute-done.3.other = f32[5,16,128]{2,1,0:T(8,128)S(1)} collective-permute-done((f32[5,16,128]{2,1,0:T(8,128)S(1)}, f32[5,16,128]{2,1,0:T(8,128)S(1)}, u32[]{:S(2)}, u32[]{:S(2)}) %collective-permute-start.3) | collective-permute-done | bytes 40992 | tf_op jit(solution)/shard_map/ppermute | solution.py:510
  17.3 0.8 %shard_map.88 = f32[2,25,16,128]{3,2,1,0:T(8,128)} custom-call(f32[5,16,128]{2,1,0:T(8,128)S(1)} %get-tuple-element.55.own, f32[5,16,128]{2,1,0:T(8,128)S(1)} %collective-permute-done.3.other, f32[2,25,16,128]{3,2,1,0:T(8,128)S(1)} %get-tuple-element.65.base, f32[25,16,128]{2,1,0:T(8,128)S(1)} %get-tuple-element.66.gain), custom_call_target="tpu_custom_call" | custom-call | flops 512000 | bytes 1105920 | tf_op jit(solution)/shard_map/pallas_call | solution.py:21
  (1 shorter events, 0.0 us)
Async XLA Ops:
  1.6 4.4 %collective-permute-start.1 = (f32[2,2,16,128]{3,2,1,0:T(8,128)S(1)}, f32[2,2,16,128]{3,2,1,0:T(8,128)S(1)}, u32[]{:S(2)}, u32[]{:S(2)}) collective-permute-start(f32[2,2,16,128]{3,2,1,0:T(8,128)S(1)} %get-tuple-element.49), channel_id=1, source_target_pairs={{0,4},{4,0},{8,12},{12,8},{16,20},{20,16},{24,28},{28,24},{1,5},{5... | collective-permute-start | bytes 98312 | tf_op jit(solution)/shard_map/ppermute | solution.py:485
  2.1 5.2 %collective-permute-start = (f32[2,2,16,128]{3,2,1,0:T(8,128)S(1)}, f32[2,2,16,128]{3,2,1,0:T(8,128)S(1)}, u32[]{:S(2)}, u32[]{:S(2)}) collective-permute-start(f32[2,2,16,128]{3,2,1,0:T(8,128)S(1)} %get-tuple-element.43), channel_id=1, source_target_pairs={{0,28},{4,8},{8,4},{12,16},{16,12},{20,24},{24,20},{28,0},{1,29},{... | collective-permute-start | bytes 98312 | tf_op jit(solution)/shard_map/ppermute | solution.py:484
  7.7 4.5 %collective-permute-start.2 = (f32[10,16,128]{2,1,0:T(8,128)S(1)}, f32[10,16,128]{2,1,0:T(8,128)S(1)}, u32[]{:S(2)}, u32[]{:S(2)}) collective-permute-start(f32[10,16,128]{2,1,0:T(8,128)S(1)} %get-tuple-element.54.own), channel_id=1, source_target_pairs={{0,1},{1,0},{2,3},{3,2},{4,5},{5,4},{6,7},{7,6},{8,9},{9,8},{10,11... | collective-permute-start | bytes 245768 | tf_op jit(solution)/shard_map/ppermute | solution.py:506
  12.3 5.0 %collective-permute-start.3 = (f32[5,16,128]{2,1,0:T(8,128)S(1)}, f32[5,16,128]{2,1,0:T(8,128)S(1)}, u32[]{:S(2)}, u32[]{:S(2)}) collective-permute-start(f32[5,16,128]{2,1,0:T(8,128)S(1)} %get-tuple-element.55.own), channel_id=1, source_target_pairs={{0,2},{1,3},{2,0},{3,1},{4,6},{5,7},{6,4},{7,5},{8,10},{9,11},{10,... | collective-permute-start | bytes 122888 | tf_op jit(solution)/shard_map/ppermute | solution.py:510

commit v7 on v6

--- a/solution.py
+++ b/solution.py
@@ -179,7 +179,7 @@
     levels, _, width = mask.shape
     tracers = tracer.shape[0]
     assert tracers == 2
-    pairs = [(tracer_in, tracer, 0), (east_in, east, 1), (bottom_in, bottom, 2), (mask_in, mask, 3), (mixing_in, mixing, 3)]
+    pairs = [(bottom_in, bottom, 2), (tracer_in, tracer, 0), (east_in, east, 1), (mask_in, mask, 3), (mixing_in, mixing, 3)]
     pairs += [(north_in, north, 4), (vertical_in, vertical, 5), (mixing_vertical_in, mixing_vertical, 5)]
     copies = [pltpu.make_async_copy(source, target, sems.at[n]) for source, target, n in pairs]
     for copy in copies:
@@ -193,13 +193,13 @@
         found[j, t] = pair[0]
         west_tiles[j, t], east_tiles[j, t] = pair
 
-    copies[0].wait()
     copies[1].wait()
+    copies[2].wait()
     for t, part in enumerate(slots):
         for i in range(tracers):
             find(i, t, window_tiles(lambda k: tracer[i, k], part))
         find(tracers + 2, t, window_tiles(lambda k: east[k], part))
-    copies[2].wait()
+    copies[0].wait()
     two_blocks[0].wait()
     copies[5].wait()
     floor = bottom[...] - lax.axis_index("gz") * levels

time: 18.2 us -> 18.2 us (level)
  no operation moved by 1% of the time
where the time goes in v7:
time: 18.2 us; the launch traced here: 18.1 us
  starting transfers between devices  8.69 us (48%)
  Pallas kernels  4.7 us (26%)
  waiting for transfers between devices  4.63 us (25%)
    pallas_call x7, Pallas kernels, call(): pl.pallas_call(kernel, out_shape=outs, in_specs=in_specs or [VMEM] * len(...  4.7 us
    ppermute x1, starting transfers between devices, local(): far = lax.ppermute(to_far, 'gx', far_pairs)  3.56 us
    ppermute x1, starting transfers between devices, local(): beyond = lax.ppermute(merged, 'gz', [(i, i ^ 2) for i in range(4)])  2.81 us
    ppermute x1, waiting for transfers between devices, local(): other = lax.ppermute(message, 'gz', [(i, i ^ 1) for i in range(4)])  2.71 us
    ppermute x1, starting transfers between devices, local(): other = lax.ppermute(message, 'gz', [(i, i ^ 1) for i in range(4)])  1.8 us
    ppermute x1, waiting for transfers between devices, local(): beyond = lax.ppermute(merged, 'gz', [(i, i ^ 2) for i in range(4)])  1.8 us
    ppermute x1, starting transfers between devices, local(): near = lax.ppermute(to_near, 'gx', near_pairs)  0.52 us
  transfers between devices with their start and end apart: 4, of which 3 were waited for; matrix products, arithmetic and copies ran while one was open for 0% of the time, Pallas kernels for 10%

profile of v7, /device:TPU:0, one launch (start us, length us, event | category | flops | bytes accessed | tf_op | source)
XLA Modules:
  0.0 18.1 jit_solution(13664980223631754202)
XLA Ops:
  0.0 1.6 %shard_map.82 = (f32[2,25,16,128]{3,2,1,0:T(8,128)S(1)}, f32[25,16,128]{2,1,0:T(8,128)S(1)}, f32[25,16,128]{2,1,0:T(8,128)S(1)}, f32[25,16,128]{2,1,0:T(8,128)S(...) custom-call(f32[2,25,16,128]{3,2,1,0:T(8,128)} %tracer_in.1, ...), custom_call_target="tpu_custom_call" | custom-call | flops 1024000 | bytes 3547136 | tf_op jit(solution)/shard_map/pallas_call | solution.py:21
  1.6 0.5 %collective-permute-start.1 = (f32[2,2,16,128]{3,2,1,0:T(8,128)S(1)}, f32[2,2,16,128]{3,2,1,0:T(8,128)S(1)}, u32[]{:S(2)}, u32[]{:S(2)}) collective-permute-start(f32[2,2,16,128]{3,2,1,0:T(8,128)S(1)} %get-tuple-element.49), channel_id=1, source_target_pairs={{0,4},{4,0},{8,12},{12,8},{16,20},{20,16},{24,28},{28,24},{1,5},{5... | collective-permute-start | bytes 98312 | tf_op jit(solution)/shard_map/ppermute | solution.py:485
  2.1 3.6 %collective-permute-start = (f32[2,2,16,128]{3,2,1,0:T(8,128)S(1)}, f32[2,2,16,128]{3,2,1,0:T(8,128)S(1)}, u32[]{:S(2)}, u32[]{:S(2)}) collective-permute-start(f32[2,2,16,128]{3,2,1,0:T(8,128)S(1)} %get-tuple-element.43), channel_id=1, source_target_pairs={{0,28},{4,8},{8,4},{12,16},{16,12},{20,24},{24,20},{28,0},{1,29},{... | collective-permute-start | bytes 98312 | tf_op jit(solution)/shard_map/ppermute | solution.py:484
  5.7 0.3 %shard_map.83 = (f32[6,2,16,128]{3,2,1,0:T(8,128)S(1)}, f32[9,2,16,128]{3,2,1,0:T(8,128)S(1)}, f32[25,16,128]{2,1,0:T(8,128)S(1)}, f32[25,16,128]{2,1,0:T(8,128)...) custom-call(f32[25,16,128]{2,1,0:T(8,128)S(1)} %get-tuple-element.36, ...), custom_call_target="tpu_custom_call" | custom-call | flops 2560000 | bytes 2940928 | tf_op jit(solution)/shard_map/pallas_call | solution.py:21
  6.0 0.0 collective-permute-done.1.near
  6.0 1.2 %shard_map.84 = (f32[2,25,16,128]{3,2,1,0:T(8,128)S(1)}, f32[4,16,128]{2,1,0:T(8,128)S(1)}, f32[2,2,16,128]{3,2,1,0:T(8,128)S(1)}) custom-call(f32[2,25,16,128]{3,2,1,0:T(8,128)S(1)} %get-tuple-element.44.tracer, f32[25,16,128]{2,1,0:T(8,128)S(1)} %get-tuple-element.45.mixing, f32[25,16,128]{2,1,0:T(8,128)S(1)} %get-tuple-element.46.east, ...), custom_call_target="tpu_custom_call" | custom-call | flops 5120000 | bytes 2342912 | tf_op jit(solution)/shard_map/pallas_call | solution.py:21
  7.2 0.1 collective-permute-done.far
  7.3 0.5 %shard_map.85 = (f32[2,2,16,128]{3,2,1,0:T(8,128)S(1)}, f32[10,16,128]{2,1,0:T(8,128)S(1)}) custom-call(f32[6,2,16,128]{3,2,1,0:T(8,128)S(1)} %get-tuple-element.41.far_tiles, f32[9,2,16,128]{3,2,1,0:T(8,128)S(1)} %get-tuple-element.42.far_moved, f32[2,2,16,128]{3,2,1,0:T(8,128)S(1)} %collective-permute-done.far, ...), custom_call_target="tpu_custom_call" | custom-call | flops 1024000 | bytes 1318912 | tf_op jit(solution)/shard_map/pallas_call | solution.py:21
  7.8 1.8 %collective-permute-start.2 = (f32[10,16,128]{2,1,0:T(8,128)S(1)}, f32[10,16,128]{2,1,0:T(8,128)S(1)}, u32[]{:S(2)}, u32[]{:S(2)}) collective-permute-start(f32[10,16,128]{2,1,0:T(8,128)S(1)} %get-tuple-element.54.own), channel_id=1, source_target_pairs={{0,1},{1,0},{2,3},{3,2},{4,5},{5,4},{6,7},{7,6},{8,9},{9,8},{10,11... | collective-permute-start | bytes 245768 | tf_op jit(solution)/shard_map/ppermute | solution.py:506
  9.6 2.7 %collective-permute-done.2.other = f32[10,16,128]{2,1,0:T(8,128)S(1)} collective-permute-done((f32[10,16,128]{2,1,0:T(8,128)S(1)}, f32[10,16,128]{2,1,0:T(8,128)S(1)}, u32[]{:S(2)}, u32[]{:S(2)}) %collective-permute-start.2) | collective-permute-done | bytes 81952 | tf_op jit(solution)/shard_map/ppermute | solution.py:506
  12.3 2.8 %collective-permute-start.3 = (f32[5,16,128]{2,1,0:T(8,128)S(1)}, f32[5,16,128]{2,1,0:T(8,128)S(1)}, u32[]{:S(2)}, u32[]{:S(2)}) collective-permute-start(f32[5,16,128]{2,1,0:T(8,128)S(1)} %get-tuple-element.55.own), channel_id=1, source_target_pairs={{0,2},{1,3},{2,0},{3,1},{4,6},{5,7},{6,4},{7,5},{8,10},{9,11},{10,... | collective-permute-start | bytes 122888 | tf_op jit(solution)/shard_map/ppermute | solution.py:510
  15.1 0.4 %shard_map.87 = (f32[2,25,16,128]{3,2,1,0:T(8,128)S(1)}, f32[25,16,128]{2,1,0:T(8,128)S(1)}) custom-call(f32[2,25,16,128]{3,2,1,0:T(8,128)S(1)} %get-tuple-element.51.lateral, f32[2,2,16,128]{3,2,1,0:T(8,128)S(1)} %get-tuple-element.56.edges, f32[25,16,128]{2,1,0:T(8,128)S(1)} %get-tuple-element.57.down, f32[25,16,128]{2,1,0:T(8,128)S(1)} %get-tuple-element.58.up, ...), custom_call_target="tpu_custom_call" | custom-call | flops 2048000 | bytes 2514944 | tf_op jit(solution)/shard_map/pallas_call | solution.py:21
  15.5 1.8 %collective-permute-done.3.other = f32[5,16,128]{2,1,0:T(8,128)S(1)} collective-permute-done((f32[5,16,128]{2,1,0:T(8,128)S(1)}, f32[5,16,128]{2,1,0:T(8,128)S(1)}, u32[]{:S(2)}, u32[]{:S(2)}) %collective-permute-start.3) | collective-permute-done | bytes 40992 | tf_op jit(solution)/shard_map/ppermute | solution.py:510
  17.3 0.8 %shard_map.88 = f32[2,25,16,128]{3,2,1,0:T(8,128)} custom-call(f32[5,16,128]{2,1,0:T(8,128)S(1)} %get-tuple-element.55.own, f32[5,16,128]{2,1,0:T(8,128)S(1)} %collective-permute-done.3.other, f32[2,25,16,128]{3,2,1,0:T(8,128)S(1)} %get-tuple-element.65.base, f32[25,16,128]{2,1,0:T(8,128)S(1)} %get-tuple-element.66.gain), custom_call_target="tpu_custom_call" | custom-call | flops 512000 | bytes 1105920 | tf_op jit(solution)/shard_map/pallas_call | solution.py:21
  (1 shorter events, 0.0 us)
Async XLA Ops:
  1.6 4.4 %collective-permute-start.1 = (f32[2,2,16,128]{3,2,1,0:T(8,128)S(1)}, f32[2,2,16,128]{3,2,1,0:T(8,128)S(1)}, u32[]{:S(2)}, u32[]{:S(2)}) collective-permute-start(f32[2,2,16,128]{3,2,1,0:T(8,128)S(1)} %get-tuple-element.49), channel_id=1, source_target_pairs={{0,4},{4,0},{8,12},{12,8},{16,20},{20,16},{24,28},{28,24},{1,5},{5... | collective-permute-start | bytes 98312 | tf_op jit(solution)/shard_map/ppermute | solution.py:485
  2.1 5.2 %collective-permute-start = (f32[2,2,16,128]{3,2,1,0:T(8,128)S(1)}, f32[2,2,16,128]{3,2,1,0:T(8,128)S(1)}, u32[]{:S(2)}, u32[]{:S(2)}) collective-permute-start(f32[2,2,16,128]{3,2,1,0:T(8,128)S(1)} %get-tuple-element.43), channel_id=1, source_target_pairs={{0,28},{4,8},{8,4},{12,16},{16,12},{20,24},{24,20},{28,0},{1,29},{... | collective-permute-start | bytes 98312 | tf_op jit(solution)/shard_map/ppermute | solution.py:484
  7.8 4.5 %collective-permute-start.2 = (f32[10,16,128]{2,1,0:T(8,128)S(1)}, f32[10,16,128]{2,1,0:T(8,128)S(1)}, u32[]{:S(2)}, u32[]{:S(2)}) collective-permute-start(f32[10,16,128]{2,1,0:T(8,128)S(1)} %get-tuple-element.54.own), channel_id=1, source_target_pairs={{0,1},{1,0},{2,3},{3,2},{4,5},{5,4},{6,7},{7,6},{8,9},{9,8},{10,11... | collective-permute-start | bytes 245768 | tf_op jit(solution)/shard_map/ppermute | solution.py:506
  12.3 5.0 %collective-permute-start.3 = (f32[5,16,128]{2,1,0:T(8,128)S(1)}, f32[5,16,128]{2,1,0:T(8,128)S(1)}, u32[]{:S(2)}, u32[]{:S(2)}) collective-permute-start(f32[5,16,128]{2,1,0:T(8,128)S(1)} %get-tuple-element.55.own), channel_id=1, source_target_pairs={{0,2},{1,3},{2,0},{3,1},{4,6},{5,7},{6,4},{7,5},{8,10},{9,11},{10,... | collective-permute-start | bytes 122888 | tf_op jit(solution)/shard_map/ppermute | solution.py:510
